TPU v7x, 128 devices: a whole 4x4x4 slice. The times are simulated.
128 devices in a mesh: gx: 16 (over z, x), gy: 8 (over y, core).
Axes of the slice: x: 4, y: 4, z: 4, core: 2. Of those that a mesh axis runs over, the one named last changes fastest.
Arguments:
- gradient: float32 [137, 512, 1024], P(None, 'gx', 'gy'), may hold values from -6 to 6
- coupling: float32 [137, 137], replicated
- transport: bfloat16 [137, 5, 512, 1024], P(None, None, 'gx', 'gy'), may hold values from 0.049804688 to 0.44921875
- obs_jacobian: bfloat16 [137, 1048576], P(None, ('gx', 'gy')), may hold values from -0.5 to 0.5
- send_cols: int32 [128, 16384], P(('gx', 'gy')), may hold values from -1 to 4095, as said below
- obs_slots: int32 [4, 1048576], P(None, ('gx', 'gy')), may hold values from 0 to 16383, as said below
- obs_weight: float32 [4, 1048576], P(None, ('gx', 'gy')), may hold values from 0.1 to 1
- obs_inst: int32 [1048576], P(('gx', 'gy')), may hold values from 0 to 31, as said below
- innovation: float32 [1048576], P(('gx', 'gy')), may hold values from -6 to 6
- valid_count: int32 [128], P(('gx', 'gy')), may hold values from 2048 to 8192
Outputs:
- sensitivity: float32 [137, 512, 1024], P(None, 'gx', 'gy')
- impact: float32 [1048576], P(('gx', 'gy'))
- inst_total: float32 [32], replicated
Inputs may be any that keep to these rules, and one draw needn't show every extreme that they name: `send_cols`: an entry is -1 exactly in the slots beyond a live count of the pair (device, owner); live counts lie between 32 and 128, and reach 128 for some pair. `obs_slots`: every entry names a slot that is not empty in the holder's send_cols for this owner. `obs_inst`: each owner holds observations of four instruments of one group.
All inputs are finite; a program needn't handle non-finite values.
Results may differ from a plain program's by a relative error of at most 0.0032.
Values may be sent and summed in bfloat16 or wider, within the bound.
A program may use at most 256 MiB of HBM per device.

v0:
```python
import jax
import jax.numpy as jnp
from jax import lax
from jax.sharding import PartitionSpec as P

NI = 32
STEPS = 2


def padded_2(x, sides, width):
    for axis, dim in sides:
        size, length = (lax.axis_size(axis), x.shape[dim])
        up = [(i, (i + 1) % size) for i in range(size - 1)]
        down = [(j, i) for i, j in up]
        last = lax.slice_in_dim(x, length - width, length, axis=dim)
        leading = lax.slice_in_dim(x, 0, width, axis=dim)
        before = lax.ppermute(last, axis, up)
        after = lax.ppermute(leading, axis, down)
        x = jnp.concatenate([before, x, after], axis=dim)
    return x


def vertical_mix(sensitivity, coupling):
    return jnp.einsum("kl,kxy->lxy", coupling, sensitivity, precision=lax.Precision.HIGHEST)


def spread(padded, coef_pad):
    weights = coef_pad.astype(jnp.float32)
    center = weights[..., 0, 1:-1, 1:-1] * padded[..., 1:-1, 1:-1]
    east = (weights[..., 1, :, :] * padded)[..., :-2, 1:-1]
    west = (weights[..., 2, :, :] * padded)[..., 2:, 1:-1]
    north = (weights[..., 3, :, :] * padded)[..., 1:-1, :-2]
    south = (weights[..., 4, :, :] * padded)[..., 1:-1, 2:]
    return center + east + west + north + south


def extend(sensitivity, rim_depth):
    return padded_2(sensitivity, (("gx", 1), ("gy", 2)), rim_depth)


def deliver(outgoing):
    return lax.all_to_all(outgoing, ("gx", "gy"), split_axis=1, concat_axis=1, tiled=True)


def transport_steps(gradient, coupling, transport):
    sensitivity = gradient
    rim_depth = 1
    coef_wide = padded_2(transport, (("gx", 2), ("gy", 3)), rim_depth)
    for repeat in range(STEPS):
        sensitivity = spread(extend(vertical_mix(sensitivity, coupling), 1), coef_wide)
    return sensitivity


def body(
    gradient,
    coupling,
    transport,
    obs_jacobian,
    send_cols,
    obs_slots,
    obs_weight,
    obs_inst,
    innovation,
    valid_count,
):
    sensitivity = transport_steps(gradient, coupling, transport)
    rows_x = gradient.shape[1]
    rows_y = gradient.shape[2]
    rounded = sensitivity.astype(jnp.bfloat16).reshape(sensitivity.shape[0], rows_x * rows_y)
    column_ids = send_cols[0]
    picked = jnp.take(rounded, jnp.maximum(column_ids, 0), axis=1)
    picked = jnp.where(column_ids[None, :] >= 0, picked, jnp.zeros_like(picked))
    received = deliver(picked)
    gathered = jnp.take(received, obs_slots, axis=1)
    interp = jnp.sum(obs_weight[None] * gathered.astype(jnp.float32), axis=1)
    sens_obs = jnp.sum(obs_jacobian.astype(jnp.float32) * interp, axis=0)
    active = jnp.arange(obs_slots.shape[1]) < valid_count[0]
    values = innovation * sens_obs
    impact = jnp.where(active, values, jnp.zeros_like(values))
    onehot = (obs_inst[None, :] == jnp.arange(NI, dtype=jnp.int32)[:, None]).astype(jnp.float32)
    instrument_part = jnp.dot(onehot, impact, precision=lax.Precision.HIGHEST)
    inst_total = lax.psum(instrument_part, ("gx", "gy"))
    return (sensitivity, impact, inst_total)


def solution(mesh):
    placed = (
        P(None, "gx", "gy"),
        P(),
        P(None, None, "gx", "gy"),
        P(None, ("gx", "gy")),
        P(("gx", "gy"), None),
        P(None, ("gx", "gy")),
        P(None, ("gx", "gy")),
        P(("gx", "gy")),
        P(("gx", "gy")),
        P(("gx", "gy")),
    )
    return jax.shard_map(
        body,
        mesh=mesh,
        in_specs=placed,
        out_specs=(P(None, "gx", "gy"), P(("gx", "gy")), P()),
        check_vma=False,
    )
```

profile of v0, /device:TPU:1, one launch (start us, length us, event | category | flops | bytes accessed | tf_op | source)
XLA Modules:
  0.0 543.0 jit_solution(17886422047429345678)
XLA Ops:
  2.3 4.3 fusion.17
  6.6 3.9 collective-permute-start.4
  14.2 4.0 collective-permute-start
  19.8 3.0 fusion.35
  22.8 3.0 copy.38
  25.8 4.6 collective-permute-start.6
  41.0 5.2 constant_dynamic-update-slice_fusion.1
  46.2 6.5 %fusion.32 = (bf16[137,5,34,1]{3,0,2,1:T(8,128)(2,1)}, bf16[137,5,34,1]{3,0,2,1:T(8,128)(2,1)}) fusion(bf16[137,5,34,128]{3,0,2,1:T(8,128)(2,1)S(1)} %constant_dynamic-update-slice_fusion), kind=kLoop, calls=%fused_computation.63 | loop fusion | bytes 186320 | tf_op jit(solution)/shard_map/slice | solution.py:15
  52.7 6.5 %copy.32 = bf16[137,5,34,1]{0,2,3,1:T(8,128)(2,1)S(1)} copy(bf16[137,5,34,1]{3,0,2,1:T(8,128)(2,1)} %get-tuple-element.20) | data formatting | bytes 93160 | tf_op jit(solution)/shard_map/slice | solution.py:15
  62.1 6.5 %copy.33 = bf16[137,5,34,1]{0,2,3,1:T(8,128)(2,1)S(1)} copy(bf16[137,5,34,1]{3,0,2,1:T(8,128)(2,1)} %get-tuple-element.21) | data formatting | bytes 93160 | tf_op jit(solution)/shard_map/slice | solution.py:16
  70.5 6.6 %pad_maximum_fusion = f32[137,34,130]{2,0,1:T(8,128)} fusion(f32[137,34,1]{2,0,1:T(8,128)} %copy.41, f32[137,1,128]{2,0,1:T(8,128)S(1)} %collective-permute-done.5, f32[137,32,128]{2,0,1:T(8,128)} %copy-done.7, f32[137,1,128]{2,0,1:T(8,128)S(1)} %collective-permute-done.4, f32[137,34,1]{2,0,1:T(8,128)} %copy.40), kind=kLoop, calls=%fused_computation.8 | loop fusion | flops 2422160 | bytes 4844320 | tf_op jit(solution)/shard_map/concatenate | solution.py:19
  77.1 4.8 copy.34
  81.9 4.8 copy.35
  86.7 14.5 %convert_bitcast_fusion.2 = (f32[137,34,130]{2,0,1:T(8,128)}, f32[137,34,130]{2,0,1:T(8,128)}, f32[137,34,130]{2,0,1:T(8,128)}, f32[137,34,130]{2,0,1:T(8,128)}) fusion(bf16[137,5,34,1]{3,0,2,1:T(8,128)(2,1)} %copy.35, bf16[137,5,34,128]{3,0,2,1:T(8,128)(2,1)} %copy-done.2, bf16[137,5,34,1]{3,0,2,1:T(8,128)(2,1)} %copy.34), kind=kLoop, calls=%fused_computation.7 | loop fusion | flops 14532960 | bytes 15744040 | tf_op jit(solution)/shard_map/squeeze | solution.py:30
  103.3 14.1 %fusion.23 = f32[137,32,128]{2,0,1:T(8,128)S(1)} fusion(f32[137,34,130]{2,0,1:T(8,128)} %pad_maximum_fusion, f32[137,32,128]{2,0,1:T(8,128)S(1)} %copy-done.8, bf16[137,1,32,128]{3,0,2,1:T(8,128)(2,1)S(1)} %pad_maximum_fusion.6, f32[137,34,130]{2,0,1:T(8,128)} %get-tuple-element.19, f32[137,34,130]{2,0,1:T(8,128)} %get-tuple-element.17, ...), kind=kOutput, calls=%fused_computation.42 | convolution fusion | flops 928145408 | bytes 24560964 | tf_op jit(solution)/shard_map/kl,kxy->lxy/dot_general | solution.py:24
  117.4 4.3 collective-permute-start.8
  123.3 4.2 collective-permute-done.9
  127.6 3.1 fusion.34
  133.7 4.6 collective-permute-start.10
  148.8 5.3 pad_maximum_fusion.1
  154.1 8.9 %fusion.30 = (bf16[137,32,128]{2,0,1:T(8,128)(2,1)S(1)}, f32[137,32,128]{2,0,1:T(8,128)}) fusion(f32[137,34,130]{2,0,1:T(8,128)S(1)} %pad_maximum_fusion.1, f32[137,34,130]{2,0,1:T(8,128)} %get-tuple-element.19, f32[137,34,130]{2,0,1:T(8,128)} %get-tuple-element.17, f32[137,34,130]{2,0,1:T(8,128)} %get-tuple-element.18, ...), kind=kLoop, calls=%fused_computation.62 | loop fusion | flops 6172672 | bytes 24690688 | tf_op jit(solution)/shard_map/convert_element_type | solution.py:69
  165.3 64.9 %gather_fusion = bf16[16384,137]{1,0:T(8,128)(2,1)} fusion(bf16[137,4096]{0,1:T(8,128)(2,1)S(1)} %bitcast.53, s32[16384]{0:T(1024)S(1)} %broadcast_clamp_fusion.1), kind=kCustom, calls=%fused_computation | custom fusion | bytes 9043968 | tf_op jit(solution)/shard_map/jit(_take)/gather | solution.py:71
  230.2 9.5 %copy.50 = bf16[137,128,128]{2,0,1:T(8,128)(2,1)} copy(bf16[137,128,128]{0,2,1:T(8,128)(2,1)} %bitcast.55) | data formatting | bytes 8978432 | tf_op jit(solution)/shard_map/jit(_take)/gather | solution.py:71
  239.6 5.2 select_select_fusion
  244.8 16.8 %all-to-all-start = ((bf16[137,128,128]{2,0,1:T(8,128)(2,1)}), bf16[137,128,128]{2,0,1:T(8,128)(2,1)}, u32[]{:S(2)}, u32[]{:S(2)}) async-start(bf16[137,128,128]{2,0,1:T(8,128)(2,1)} %select_select_fusion), calls=%async_computation | async-start | bytes 9437184 | tf_op jit(solution)/shard_map/all_to_all | solution.py:42
  261.7 5.6 %copy.47 = bf16[137,8192]{0,1:T(8,128)(2,1)} copy(bf16[137,8192]{1,0:T(8,128)(2,1)} %param.13) | data formatting | bytes 4489216 | tf_op args[3]
  268.1 51.9 %all-to-all-done = bf16[137,128,128]{2,0,1:T(8,128)(2,1)} async-done(((bf16[137,128,128]{2,0,1:T(8,128)(2,1)}), bf16[137,128,128]{2,0,1:T(8,128)(2,1)}, u32[]{:S(2)}, u32[]{:S(2)}) %all-to-all-start) | async-done | bytes 4489248 | tf_op jit(solution)/shard_map/all_to_all | solution.py:42
  320.0 9.2 %copy.51 = bf16[137,128,128]{0,2,1:T(8,128)(2,1)} copy(bf16[137,128,128]{2,0,1:T(8,128)(2,1)} %all-to-all-done) | data formatting | bytes 8978432 | tf_op jit(solution)/shard_map/all_to_all | solution.py:42
  329.1 125.4 %gather_fusion.1 = bf16[32768,137]{1,0:T(8,128)(2,1)} fusion(bf16[137,16384]{0,1:T(8,128)(2,1)} %bitcast.52, s32[32768]{0:T(1024)S(1)} %broadcast_clamp_fusion), kind=kCustom, calls=%fused_computation.1 | custom fusion | bytes 18087936 | tf_op jit(solution)/shard_map/jit(_take)/gather | solution.py:74
  454.6 16.5 %multiply_reduce_fusion = f32[8192,137]{1,0:T(8,128)} fusion(f32[4,8192]{1,0:T(4,128)S(1)} %copy-done.13, bf16[4,8192,137]{2,1,0:T(8,128)(2,1)} %bitcast.54, pred[4,8192]{1,0:T(4,128)(4,1)S(1)} %compare_and_fusion), kind=kLoop, calls=%fused_computation.2 | loop fusion | flops 16834560 | bytes 13631488 | tf_op jit(solution)/shard_map/reduce_sum | solution.py:75
  471.0 5.9 %fusion = f32[8192]{0:T(1024)S(1)} fusion(f32[8192,137]{1,0:T(8,128)} %multiply_reduce_fusion, bf16[137,8192]{0,1:T(8,128)(2,1)} %copy.47), kind=kLoop, calls=%fused_computation.4 | loop fusion | flops 3358720 | bytes 6766592 | tf_op jit(solution)/shard_map/reduce_sum | solution.py:76
  479.6 62.9 %psum.7 = f32[32]{0:T(128)} all-reduce(f32[32]{0:T(128)S(1)} %convolution_bitcast_fusion), channel_id=1, replica_groups=mesh['gx'=16,'gy'=8] {'gx','gy'}, use_global_device_ids=true, to_apply=%region_2.3 | all-reduce | flops 32 | bytes 256 | tf_op jit(solution)/shard_map/psum | solution.py:82
  (80 shorter events, 44.6 us)
Async XLA Ops:
  0.6 1.6 copy-start
  6.5 13.0 %copy-start.7 = (f32[137,32,128]{2,0,1:T(8,128)}, f32[137,32,128]{2,0,1:T(8,128)S(1)}, u32[]{:S(2)}) copy-start(f32[137,32,128]{2,0,1:T(8,128)S(1)} %fusion.17) | copy-start | bytes 6733828
  6.6 13.0 %collective-permute-start.4 = (f32[137,1,128]{2,0,1:T(8,128)S(1)}, f32[137,1,128]{2,0,1:T(8,128)S(1)}, u32[]{:S(2)}, u32[]{:S(2)}) collective-permute-start(f32[137,1,128]{2,0,1:T(8,128)S(1)} %get-tuple-element.30), channel_id=1, source_target_pairs={{0,8},{8,16},{16,24},{24,32},{32,40},{40,48},{48,56},{56,64},{64,7... | collective-permute-start | bytes 210440 | tf_op jit(solution)/shard_map/ppermute | solution.py:17
  10.5 9.0 %collective-permute-start.5 = (f32[137,1,128]{2,0,1:T(8,128)S(1)}, f32[137,1,128]{2,0,1:T(8,128)S(1)}, u32[]{:S(2)}, u32[]{:S(2)}) collective-permute-start(f32[137,1,128]{2,0,1:T(8,128)S(1)} %get-tuple-element.31), channel_id=1, source_target_pairs={{8,0},{16,8},{24,16},{32,24},{40,32},{48,40},{56,48},{64,56},{72,6... | collective-permute-start | bytes 210440 | tf_op jit(solution)/shard_map/ppermute | solution.py:18
  14.2 26.8 %collective-permute-start = (bf16[137,5,1,128]{3,0,2,1:T(8,128)(2,1)S(1)}, bf16[137,5,1,128]{3,0,2,1:T(8,128)(2,1)S(1)}, u32[]{:S(2)}, u32[]{:S(2)}) collective-permute-start(bf16[137,5,1,128]{3,0,2,1:T(8,128)(2,1)S(1)} %copy.63), channel_id=1, source_target_pairs={{0,8},{8,16},{16,24},{24,32},{32,40},{40,48},{48,56},{56,64},{64,7... | collective-permute-start | bytes 526088 | tf_op jit(solution)/shard_map/ppermute | solution.py:17
  18.3 27.9 %collective-permute-start.1 = (bf16[137,5,1,128]{3,0,2,1:T(8,128)(2,1)S(1)}, bf16[137,5,1,128]{3,0,2,1:T(8,128)(2,1)S(1)}, u32[]{:S(2)}, u32[]{:S(2)}) collective-permute-start(bf16[137,5,1,128]{3,0,2,1:T(8,128)(2,1)S(1)} %copy.64), channel_id=1, source_target_pairs={{8,0},{16,8},{24,16},{32,24},{40,32},{48,40},{56,48},{64,56},{72,6... | collective-permute-start | bytes 526088 | tf_op jit(solution)/shard_map/ppermute | solution.py:18
  22.8 12.5 %copy-start.12 = (s32[1,16384]{1,0:T(1,128)S(1)}, s32[1,16384]{1,0:T(1,128)}, u32[]{:S(2)}) copy-start(s32[1,16384]{1,0:T(1,128)} %param.14) | copy-start | bytes 196612
  25.8 9.6 %collective-permute-start.6 = (f32[137,34,1]{0,2,1:T(1,128)S(1)}, f32[137,34,1]{0,2,1:T(1,128)S(1)}, u32[]{:S(2)}, u32[]{:S(2)}) collective-permute-start(f32[137,34,1]{0,2,1:T(1,128)S(1)} %copy.38), channel_id=1, source_target_pairs={{0,1},{1,2},{2,3},{3,4},{4,5},{5,6},{6,7},{8,9},{9,10},{10,11},{11... | collective-permute-start | bytes 55904 | tf_op jit(solution)/shard_map/ppermute | solution.py:17
  33.4 5.3 collective-permute-start.7
  46.2 6.5 %copy-start.2 = (bf16[137,5,34,128]{3,0,2,1:T(8,128)(2,1)}, bf16[137,5,34,128]{3,0,2,1:T(8,128)(2,1)S(1)}, u32[]{:S(2)}) copy-start(bf16[137,5,34,128]{3,0,2,1:T(8,128)(2,1)S(1)} %constant_dynamic-update-slice_fusion) | copy-start | bytes 17886724
  59.2 17.9 %collective-permute-start.2 = (bf16[137,5,34,1]{0,2,3,1:T(8,128)(2,1)S(1)}, bf16[137,5,34,1]{0,2,3,1:T(8,128)(2,1)S(1)}, u32[]{:S(2)}, u32[]{:S(2)}) collective-permute-start(bf16[137,5,34,1]{0,2,3,1:T(8,128)(2,1)S(1)} %copy.32), channel_id=1, source_target_pairs={{0,1},{1,2},{2,3},{3,4},{4,5},{5,6},{6,7},{8,9},{9,10},{10,11},{11... | collective-permute-start | bytes 139748 | tf_op jit(solution)/shard_map/ppermute | solution.py:17
  68.6 13.3 %collective-permute-start.3 = (bf16[137,5,34,1]{0,2,3,1:T(8,128)(2,1)S(1)}, bf16[137,5,34,1]{0,2,3,1:T(8,128)(2,1)S(1)}, u32[]{:S(2)}, u32[]{:S(2)}) collective-permute-start(bf16[137,5,34,1]{0,2,3,1:T(8,128)(2,1)S(1)} %copy.33), channel_id=1, source_target_pairs={{1,0},{2,1},{3,2},{4,3},{5,4},{6,5},{7,6},{9,8},{10,9},{11,10},{12... | collective-permute-start | bytes 139748 | tf_op jit(solution)/shard_map/ppermute | solution.py:18
  86.7 14.5 %copy-start.3 = (bf16[137,5,34,1]{3,0,2,1:T(8,128)(2,1)S(1)}, bf16[137,5,34,1]{3,0,2,1:T(8,128)(2,1)}, u32[]{:S(2)}) copy-start(bf16[137,5,34,1]{3,0,2,1:T(8,128)(2,1)} %copy.34) | copy-start | bytes 139744
  86.7 14.5 %copy-start.4 = (bf16[137,5,34,1]{3,0,2,1:T(8,128)(2,1)S(1)}, bf16[137,5,34,1]{3,0,2,1:T(8,128)(2,1)}, u32[]{:S(2)}) copy-start(bf16[137,5,34,1]{3,0,2,1:T(8,128)(2,1)} %copy.35) | copy-start | bytes 139744
  101.2 2.0 copy-start.8
  101.2 2.0 copy-start.10
  117.4 13.4 %copy-start.5 = (f32[137,32,128]{2,0,1:T(8,128)}, f32[137,32,128]{2,0,1:T(8,128)S(1)}, u32[]{:S(2)}) copy-start(f32[137,32,128]{2,0,1:T(8,128)S(1)} %fusion.23) | copy-start | bytes 6733828
  117.4 5.9 %collective-permute-start.8 = (f32[137,1,128]{2,0,1:T(8,128)S(1)}, f32[137,1,128]{2,0,1:T(8,128)S(1)}, u32[]{:S(2)}, u32[]{:S(2)}) collective-permute-start(f32[137,1,128]{2,0,1:T(8,128)S(1)} %get-tuple-element.28), channel_id=1, source_target_pairs={{0,8},{8,16},{16,24},{24,32},{32,40},{40,48},{48,56},{56,64},{64,7... | collective-permute-start | bytes 210440 | tf_op jit(solution)/shard_map/ppermute | solution.py:17
  121.7 5.8 %collective-permute-start.9 = (f32[137,1,128]{2,0,1:T(8,128)S(1)}, f32[137,1,128]{2,0,1:T(8,128)S(1)}, u32[]{:S(2)}, u32[]{:S(2)}) collective-permute-start(f32[137,1,128]{2,0,1:T(8,128)S(1)} %get-tuple-element.29), channel_id=1, source_target_pairs={{8,0},{16,8},{24,16},{32,24},{40,32},{48,40},{56,48},{64,56},{72,6... | collective-permute-start | bytes 210440 | tf_op jit(solution)/shard_map/ppermute | solution.py:18
  133.7 9.9 %collective-permute-start.10 = (f32[137,34,1]{0,2,1:T(1,128)S(1)}, f32[137,34,1]{0,2,1:T(1,128)S(1)}, u32[]{:S(2)}, u32[]{:S(2)}) collective-permute-start(f32[137,34,1]{0,2,1:T(1,128)S(1)} %copy.43), channel_id=1, source_target_pairs={{0,1},{1,2},{2,3},{3,4},{4,5},{5,6},{6,7},{8,9},{9,10},{10,11},{11... | collective-permute-start | bytes 55904 | tf_op jit(solution)/shard_map/ppermute | solution.py:17
  141.3 5.3 collective-permute-start.11
  148.8 5.3 copy-start.6
  244.8 16.8 %copy-start.11 = (s32[4,8192]{1,0:T(4,128)S(1)}, s32[4,8192]{1,0:T(4,128)}, u32[]{:S(2)}) copy-start(s32[4,8192]{1,0:T(4,128)} %param.15) | copy-start | bytes 393220
  244.8 75.1 %all-to-all-start = ((bf16[137,128,128]{2,0,1:T(8,128)(2,1)}), bf16[137,128,128]{2,0,1:T(8,128)(2,1)}, u32[]{:S(2)}, u32[]{:S(2)}) async-start(bf16[137,128,128]{2,0,1:T(8,128)(2,1)} %select_select_fusion), calls=%async_computation | async-start | bytes 9437184 | tf_op jit(solution)/shard_map/all_to_all | solution.py:42
  329.1 125.5 %copy-start.13 = (f32[4,8192]{1,0:T(4,128)S(1)}, f32[4,8192]{1,0:T(4,128)}, u32[]{:S(2)}) copy-start(f32[4,8192]{1,0:T(4,128)} %param.16) | copy-start | bytes 393220
  471.0 5.9 %copy-start.14 = (f32[8192]{0:T(1024)S(1)}, f32[8192]{0:T(1024)}, u32[]{:S(2)}) copy-start(f32[8192]{0:T(1024)} %param.18) | copy-start | bytes 98308
  471.0 5.9 %copy-start.16 = (s32[8192]{0:T(1024)S(1)}, s32[8192]{0:T(1024)}, u32[]{:S(2)}) copy-start(s32[8192]{0:T(1024)} %param.17) | copy-start | bytes 98308
  471.0 6.5 %copy-start.9 = (f32[137,32,128]{2,0,1:T(8,128)S(1)}, f32[137,32,128]{2,0,1:T(8,128)}, u32[]{:S(2)}) copy-start(f32[137,32,128]{2,0,1:T(8,128)} %get-tuple-element.15) | copy-start | bytes 6733828
  471.0 71.5 %copy-start.1 = (f32[137,32,128]{2,1,0:T(8,128)S(1)}, f32[137,32,128]{2,1,0:T(8,128)}, u32[]{:S(2)}) copy-start(f32[137,32,128]{2,1,0:T(8,128)} %param.10) | copy-start | bytes 6733828
  477.0 65.6 %copy-start.15 = (f32[8192]{0:T(1024)}, f32[8192]{0:T(1024)S(1)}, u32[]{:S(2)}) copy-start(f32[8192]{0:T(1024)S(1)} %multiply_select_fusion) | copy-start | bytes 98308
where the time goes:
time: 553 us; the launch traced here: 543 us
  local copies, waits for them, and re-layouts  285 us (52%)
  other arithmetic  65.7 us (12%)
  blocking collectives  62.9 us (11%)
  waiting for transfers between devices  57.8 us (10%)
  starting transfers between devices  50.7 us (9%)
  matrix products  18.9 us (3%)
    gather x1, local copies, waits for them, and re-layouts, body(): gathered = jnp.take(received, obs_slots, axis=1)  125 us
    gather x2, local copies, waits for them, and re-layouts, body(): picked = jnp.take(rounded, jnp.maximum(column_ids, 0), axis=1)  74.4 us
    psum x1, blocking collectives, body(): inst_total = lax.psum(instrument_part, ('gx', 'gy'))  62.9 us
    all_to_all x1, waiting for transfers between devices, deliver(): lax.all_to_all(outgoing, ('gx', 'gy'), split_axis=1, concat_axis=1, tiled...  51.9 us
    slice x8, local copies, waits for them, and re-layouts, padded_2(): last = lax.slice_in_dim(x, length - width, length, axis=dim)  25.1 us
    ppermute x6, starting transfers between devices, padded_2(): before = lax.ppermute(last, axis, up)  24.3 us
    dot_general x2, matrix products, vertical_mix(): jnp.einsum('kl,kxy->lxy', coupling, sensitivity, precision=lax.Precision....  18.4 us
    all_to_all x1, starting transfers between devices, deliver(): lax.all_to_all(outgoing, ('gx', 'gy'), split_axis=1, concat_axis=1, tiled...  16.8 us
  transfers between devices with their start and end apart: 13, of which 5 were waited for; matrix products, arithmetic and copies ran while one was open for 9% of the time, Pallas kernels for 0%

commit v1 on v0

--- a/solution.py
+++ b/solution.py
@@ -1,10 +1,22 @@
 import jax
 import jax.numpy as jnp
 from jax import lax
+from jax.experimental import pallas as pl
+from jax.experimental.pallas import tpu as pltpu
 from jax.sharding import PartitionSpec as P
 
 NI = 32
 STEPS = 2
+LANES = 128
+MAIN = 128
+TAIL = 16
+BLOCK = MAIN + TAIL
+GROUP = 8
+STRIDE = 37
+MESH = pl.DeviceIdType.MESH
+VMEM = pl.BlockSpec(memory_space=pltpu.VMEM)
+SMEM = pl.BlockSpec(memory_space=pltpu.SMEM)
+MIB = 1024 * 1024
 
 
 def padded_2(x, sides, width):
@@ -38,10 +50,6 @@
     return padded_2(sensitivity, (("gx", 1), ("gy", 2)), rim_depth)
 
 
-def deliver(outgoing):
-    return lax.all_to_all(outgoing, ("gx", "gy"), split_axis=1, concat_axis=1, tiled=True)
-
-
 def transport_steps(gradient, coupling, transport):
     sensitivity = gradient
     rim_depth = 1
@@ -49,6 +57,282 @@
     for repeat in range(STEPS):
         sensitivity = spread(extend(vertical_mix(sensitivity, coupling), 1), coef_wide)
     return sensitivity
+
+
+def identity(rows, dtype):
+    row = lax.broadcasted_iota(jnp.int32, (rows, LANES), 0)
+    col = lax.broadcasted_iota(jnp.int32, (rows, LANES), 1)
+    return (row == col).astype(dtype)
+
+
+def dot_nt(a, b):
+    return lax.dot_general(a, b, (((1,), (1,)), ((), ())), preferred_element_type=jnp.float32)
+
+
+def peer(step):
+    gx, gy = lax.axis_index("gx"), lax.axis_index("gy")
+    z, x, y, core = gx // 4, lax.rem(gx, 4), gy // 2, lax.rem(gy, 2)
+    dz, dx, dy, dc = lax.rem(step, 4), lax.rem(step // 4, 4), lax.rem(step // 16, 4), step // 64
+    return (
+        lax.rem(z + dz, 4) * 4 + lax.rem(x + dx, 4),
+        lax.rem(y + dy, 4) * 2 + lax.rem(core + dc, 2),
+    )
+
+
+def exchange_kernel(levels, columns, field, received, table, ga, gb, outgoing, send_sem, recv_sem, own_sem):
+    gx, gy = lax.axis_index("gx"), lax.axis_index("gy")
+    me = gx * 8 + gy
+    ranks = received.shape[0]
+    barrier = pltpu.get_barrier_semaphore()
+
+    @pl.loop(1, ranks)
+    def _(k):
+        pl.semaphore_signal(barrier, inc=1, device_id=peer(k), device_id_type=MESH)
+
+    rows_x = field.shape[0] // levels
+    eye = identity(LANES, jnp.bfloat16)
+
+    @pl.loop(0, rows_x, unroll=4)
+    def _(x):
+        slab = field[pl.ds(x, levels, stride=rows_x), :]
+        tail = jnp.concatenate([slab[MAIN:levels], jnp.zeros((2 * MAIN - levels, LANES), jnp.float32)], axis=0)
+        base = pl.multiple_of(x * 2 * LANES, 2 * LANES)
+        table[pl.ds(base, LANES, stride=2), :] = dot_nt(eye, slab[:MAIN].astype(jnp.bfloat16))
+        table[pl.ds(base + 1, LANES, stride=2), :] = dot_nt(eye, tail.astype(jnp.bfloat16))
+
+    pick = identity(TAIL, jnp.bfloat16)
+    pl.semaphore_wait(barrier, ranks - 1)
+
+    def step_at(k):
+        return lax.rem((k + 1) * STRIDE, ranks)
+
+    def owner_at(k):
+        tx, ty = peer(step_at(k))
+        return tx * 8 + ty
+
+    def copy_for(k):
+        step = step_at(k)
+        tx, ty = peer(step)
+        return pltpu.make_async_remote_copy(
+            src_ref=outgoing.at[tx * 8 + ty],
+            dst_ref=received.at[me],
+            send_sem=send_sem.at[step],
+            recv_sem=recv_sem.at[step],
+            device_id=(tx, ty),
+            device_id_type=MESH,
+        )
+
+    def gather(k, rows, first, count):
+        base = owner_at(k) * LANES
+        for i in range(first, first + count, GROUP):
+            got = [table[pl.ds(columns[base + i + j], 2), :] for j in range(GROUP)]
+            for j in range(GROUP):
+                rows[pl.ds((i + j) * 2, 2), :] = got[j]
+
+    def pack(k, rows, next_k, next_rows):
+        owner = owner_at(k)
+        main = rows[pl.ds(0, LANES, stride=2), :].astype(jnp.bfloat16)
+        tail = rows[pl.ds(1, LANES, stride=2), :].astype(jnp.bfloat16)
+        packed = dot_nt(pick, tail)
+        gather(next_k, next_rows, 0, LANES)
+        outgoing[owner, 0:MAIN, :] = main
+        outgoing[owner, MAIN:BLOCK, :] = packed.astype(jnp.bfloat16)
+
+    gather(0, ga, 0, LANES)
+
+    @pl.loop(0, ranks // 2)
+    def _(t):
+        k = t * 2
+        pack(k, ga, k + 1, gb)
+        copy_for(k).start()
+        pack(k + 1, gb, jnp.minimum(k + 2, ranks - 1), ga)
+
+        @pl.when(k + 1 < ranks - 1)
+        def _():
+            copy_for(k + 1).start()
+
+    own = pltpu.make_async_copy(outgoing.at[me], received.at[me], own_sem)
+    own.start()
+
+    @pl.loop(0, ranks - 1)
+    def _(k):
+        copy_for(k).wait()
+
+    own.wait()
+
+
+def exchange(columns, field, ranks):
+    levels, rows_x, lanes = field.shape
+    flat = field.reshape(levels * rows_x, lanes)
+    block = jax.ShapeDtypeStruct((ranks, BLOCK, LANES), jnp.bfloat16)
+
+    def kernel(*refs):
+        exchange_kernel(levels, *refs)
+
+    return pl.pallas_call(
+        kernel,
+        out_shape=block,
+        in_specs=[SMEM, VMEM],
+        out_specs=VMEM,
+        scratch_shapes=[
+            pltpu.VMEM((rows_x * lanes * 2, LANES), jnp.float32),
+            pltpu.VMEM((2 * LANES, LANES), jnp.float32),
+            pltpu.VMEM((2 * LANES, LANES), jnp.float32),
+            pltpu.VMEM(block.shape, block.dtype),
+            pltpu.SemaphoreType.DMA((ranks,)),
+            pltpu.SemaphoreType.DMA((ranks,)),
+            pltpu.SemaphoreType.DMA,
+        ],
+        compiler_params=pltpu.CompilerParams(collective_id=1, has_side_effects=True, vmem_limit_bytes=40 * MIB),
+        name="exchange",
+    )(columns, flat)
+
+
+def impact_kernel(slots, valid, received, jac, weight, innovation, inst, impact, part, table, ga, gb):
+    levels, holders, chunks = jac.shape[0], received.shape[0], impact.shape[0]
+    eye = identity(LANES, jnp.int32) == 1
+    spread_tail = identity(TAIL, jnp.bfloat16)
+
+    @pl.loop(0, holders, unroll=8)
+    def _(h):
+        base = pl.multiple_of(h * 2 * LANES, 2 * LANES)
+        table[pl.ds(base, LANES, stride=2), :] = received[h, 0:MAIN, :].astype(jnp.float32)
+        table[pl.ds(base + 1, LANES, stride=2), :] = lax.dot_general(
+            received[h, MAIN:BLOCK, :], spread_tail, (((0,), (0,)), ((), ())), preferred_element_type=jnp.float32
+        )
+
+    part[...] = jnp.zeros_like(part)
+    lane = lax.broadcasted_iota(jnp.int32, (1, LANES), 1)
+    points = 4
+    rows_per = points * LANES
+
+    def gather(j, rows, first, count):
+        for i in range(first, first + count, GROUP):
+            got = [table[pl.ds(slots[j * rows_per + i + k], 2), :] for k in range(GROUP)]
+            for k in range(GROUP):
+                rows[pl.ds((i + k) * 2, 2), :] = got[k]
+
+    def work(j, rows, next_j, next_rows):
+        col = pl.multiple_of(j * LANES, LANES)
+        tail = jnp.concatenate(
+            [
+                jac[MAIN:levels, pl.ds(col, LANES)].astype(jnp.float32),
+                jnp.zeros((BLOCK - levels, LANES), jnp.float32),
+            ],
+            axis=0,
+        ).astype(jnp.bfloat16)
+        profile = jnp.concatenate(
+            [jac[0:MAIN, pl.ds(col, LANES)], tail, jnp.zeros((2 * MAIN - BLOCK, LANES), jnp.bfloat16)], axis=0
+        )
+        total = jnp.zeros((1, LANES), jnp.float32)
+        for c in range(points):
+            main = rows[pl.ds(c * 2 * LANES, LANES, stride=2), :].astype(jnp.bfloat16)
+            rest = rows[pl.ds(c * 2 * LANES + 1, LANES, stride=2), :].astype(jnp.bfloat16)
+            products = jnp.dot(
+                jnp.concatenate([main, rest], axis=1), profile, preferred_element_type=jnp.float32
+            )
+            gather(next_j, next_rows, c * LANES, LANES // 2)
+            diagonal = jnp.sum(jnp.where(eye, products, 0.0), axis=0, keepdims=True)
+            total = total + diagonal * weight[c : c + 1, pl.ds(col, LANES)]
+            gather(next_j, next_rows, c * LANES + LANES // 2, LANES // 2)
+        value = innovation[pl.ds(j, 1), :] * total
+        value = jnp.where(lane + j * LANES < valid[0], value, 0.0)
+        impact[pl.ds(j, 1), :] = value
+        same = lax.broadcasted_iota(jnp.int32, (NI, LANES), 0) == inst[pl.ds(j, 1), :]
+        part[...] += jnp.where(same, value, 0.0)
+
+    gather(0, ga, 0, rows_per)
+
+    @pl.loop(0, chunks // 2)
+    def _(t):
+        j = t * 2
+        work(j, ga, j + 1, gb)
+        work(j + 1, gb, jnp.minimum(j + 2, chunks - 1), ga)
+
+
+def impacts(slots, valid, received, jac, weight, innovation, inst):
+    count, holders = innovation.shape[0], received.shape[0]
+    chunks = count // LANES
+    slots = (slots * 2).reshape(4, chunks, LANES).transpose(1, 0, 2).reshape(4 * count)
+    impact, part = pl.pallas_call(
+        impact_kernel,
+        out_shape=(
+            jax.ShapeDtypeStruct((chunks, LANES), jnp.float32),
+            jax.ShapeDtypeStruct((NI, LANES), jnp.float32),
+        ),
+        in_specs=[SMEM, SMEM] + [VMEM] * 5,
+        out_specs=(VMEM, VMEM),
+        scratch_shapes=[
+            pltpu.VMEM((holders * 2 * LANES, LANES), jnp.float32),
+            pltpu.VMEM((4 * 2 * LANES, LANES), jnp.float32),
+            pltpu.VMEM((4 * 2 * LANES, LANES), jnp.float32),
+        ],
+        compiler_params=pltpu.CompilerParams(vmem_limit_bytes=48 * MIB),
+        name="impacts",
+    )(slots, valid, received, jac, weight, innovation.reshape(chunks, LANES), inst.reshape(chunks, LANES))
+    return impact.reshape(count), part
+
+
+def total_kernel(part, total, first, second, send_sem, recv_sem):
+    gx, gy = lax.axis_index("gx"), lax.axis_index("gy")
+    nx, ny = first.shape[0], second.shape[0]
+    barrier = pltpu.get_barrier_semaphore()
+    for k in range(1, ny):
+        pl.semaphore_signal(barrier, inc=1, device_id=(gx, lax.rem(gy + k, ny)), device_id_type=MESH)
+    for k in range(1, nx):
+        pl.semaphore_signal(barrier, inc=1, device_id=(lax.rem(gx + k, nx), gy), device_id_type=MESH)
+    rows = lax.dot_general(
+        jnp.ones((8, LANES), jnp.float32),
+        part[...],
+        (((1,), (1,)), ((), ())),
+        precision=lax.Precision.HIGHEST,
+        preferred_element_type=jnp.float32,
+    )
+    own = jnp.concatenate([rows, jnp.zeros((8, LANES - NI), jnp.float32)], axis=1)
+    pl.semaphore_wait(barrier, nx + ny - 2)
+
+    def share(value, slots, size, me, coords, base):
+        slots[me] = value
+        copies = [
+            pltpu.make_async_remote_copy(
+                src_ref=slots.at[me],
+                dst_ref=slots.at[me],
+                send_sem=send_sem.at[base + k],
+                recv_sem=recv_sem.at[base + k],
+                device_id=coords(lax.rem(me + k, size)),
+                device_id_type=MESH,
+            )
+            for k in range(1, size)
+        ]
+        for copy in copies:
+            copy.start()
+        for copy in copies:
+            copy.wait()
+        out = slots[0]
+        for k in range(1, size):
+            out = out + slots[k]
+        return out
+
+    across = share(own, second, ny, gy, lambda i: (gx, i), 0)
+    total[...] = share(across, first, nx, gx, lambda i: (i, gy), ny)
+
+
+def instrument_totals(part, nx, ny):
+    total = pl.pallas_call(
+        total_kernel,
+        out_shape=jax.ShapeDtypeStruct((8, LANES), jnp.float32),
+        in_specs=[VMEM],
+        out_specs=VMEM,
+        scratch_shapes=[
+            pltpu.VMEM((nx, 8, LANES), jnp.float32),
+            pltpu.VMEM((ny, 8, LANES), jnp.float32),
+            pltpu.SemaphoreType.DMA((nx + ny,)),
+            pltpu.SemaphoreType.DMA((nx + ny,)),
+        ],
+        compiler_params=pltpu.CompilerParams(collective_id=2, has_side_effects=True),
+        name="totals",
+    )(part)
+    return total[0, :NI]
 
 
 def body(
@@ -63,24 +347,14 @@
     innovation,
     valid_count,
 ):
+    nx, ny = lax.axis_size("gx"), lax.axis_size("gy")
     sensitivity = transport_steps(gradient, coupling, transport)
-    rows_x = gradient.shape[1]
-    rows_y = gradient.shape[2]
-    rounded = sensitivity.astype(jnp.bfloat16).reshape(sensitivity.shape[0], rows_x * rows_y)
-    column_ids = send_cols[0]
-    picked = jnp.take(rounded, jnp.maximum(column_ids, 0), axis=1)
-    picked = jnp.where(column_ids[None, :] >= 0, picked, jnp.zeros_like(picked))
-    received = deliver(picked)
-    gathered = jnp.take(received, obs_slots, axis=1)
-    interp = jnp.sum(obs_weight[None] * gathered.astype(jnp.float32), axis=1)
-    sens_obs = jnp.sum(obs_jacobian.astype(jnp.float32) * interp, axis=0)
-    active = jnp.arange(obs_slots.shape[1]) < valid_count[0]
-    values = innovation * sens_obs
-    impact = jnp.where(active, values, jnp.zeros_like(values))
-    onehot = (obs_inst[None, :] == jnp.arange(NI, dtype=jnp.int32)[:, None]).astype(jnp.float32)
-    instrument_part = jnp.dot(onehot, impact, precision=lax.Precision.HIGHEST)
-    inst_total = lax.psum(instrument_part, ("gx", "gy"))
-    return (sensitivity, impact, inst_total)
+    columns = jnp.maximum(send_cols[0], 0) * 2
+    received = exchange(columns, sensitivity, nx * ny)
+    impact, part = impacts(
+        obs_slots, valid_count, received, obs_jacobian, obs_weight, innovation, obs_inst
+    )
+    return (sensitivity, impact, instrument_totals(part, nx, ny))
 
 
 def solution(mesh):

time: 553 us -> 301 us (0.54); the launches traced: 543 us -> 300 us
  local copies, waits for them, and re-layouts: 285 us -> 70.4 us
  Pallas kernels: 0 us -> 133 us
  blocking collectives: 62.9 us -> 0 us
  waiting for transfers between devices: 57.8 us -> 4 us
  other arithmetic: 65.7 us -> 36.7 us
  starting transfers between devices: 50.7 us -> 35.6 us
    gather x3 -> x0, local copies, waits for them, and re-layouts: 200 us -> none  [the longest x1 125 us: body(): gathered = jnp.take(received, obs_slots, axis=1)]
    pallas_call x0 -> x3, Pallas kernels: none -> 133 us  [the longest x1 78.8 us: exchange(): pl.pallas_call(kernel, out_shape=block, in_specs=[SMEM, VMEM], out_specs=...]
    psum x1 -> x0, blocking collectives: 62.9 us -> none  [body(): inst_total = lax.psum(instrument_part, ('gx', 'gy'))]
    all_to_all x1 -> x0, waiting for transfers between devices: 51.9 us -> none  [deliver(): lax.all_to_all(outgoing, ('gx', 'gy'), split_axis=1, concat_axis=1, tiled...]
    reduce_sum x2 -> x0, other arithmetic: 22.4 us -> none  [the longest x1 16.5 us: body(): interp = jnp.sum(obs_weight[None] * gathered.astype(jnp.float32), axis=1)]
    all_to_all x1 -> x0, starting transfers between devices: 16.8 us -> none  [deliver(): lax.all_to_all(outgoing, ('gx', 'gy'), split_axis=1, concat_axis=1, tiled...]
    all_to_all x1 -> x0, local copies, waits for them, and re-layouts: 9.15 us -> none  [deliver(): lax.all_to_all(outgoing, ('gx', 'gy'), split_axis=1, concat_axis=1, tiled...]
    convert_element_type x1 -> x0, other arithmetic: 8.9 us -> none  [body(): sensitivity.astype(jnp.bfloat16)]
  transfers between devices with their start and end apart: 13 -> 12, of which waited for: 5 -> 2; matrix products, arithmetic and copies ran while one was open for 9% -> 15% of each run, Pallas kernels for 0% -> 0%
where the time goes in v1:
time: 301 us; the launch traced here: 300 us
  Pallas kernels  133 us (44%)
  local copies, waits for them, and re-layouts  70.4 us (23%)
  other arithmetic  36.7 us (12%)
  starting transfers between devices  35.6 us (12%)
  matrix products  18.5 us (6%)
  waiting for transfers between devices  4 us (1%)
    pallas_call x1, Pallas kernels, exchange(): pl.pallas_call(kernel, out_shape=block, in_specs=[SMEM, VMEM], out_specs=...  78.8 us
    pallas_call x1, Pallas kernels, impacts(): pl.pallas_call(impact_kernel, out_shape=(jax.ShapeDtypeStruct((chunks, LA...  39.3 us
    ppermute x6, starting transfers between devices, padded_2(): before = lax.ppermute(last, axis, up)  25.9 us
    slice x8, local copies, waits for them, and re-layouts, padded_2(): last = lax.slice_in_dim(x, length - width, length, axis=dim)  25.1 us
    dot_general x2, matrix products, vertical_mix(): jnp.einsum('kl,kxy->lxy', coupling, sensitivity, precision=lax.Precision....  18.5 us
    slice x4, local copies, waits for them, and re-layouts, padded_2(): leading = lax.slice_in_dim(x, 0, width, axis=dim)  14.8 us
    pallas_call x1, Pallas kernels, instrument_totals(): pl.pallas_call(total_kernel, out_shape=jax.ShapeDtypeStruct((8, LANES), j...  14.8 us
    squeeze x1, other arithmetic, spread(): east = (weights[..., 1, :, :] * padded)[..., :-2, 1:-1]  14.5 us
  transfers between devices with their start and end apart: 12, of which 2 were waited for; matrix products, arithmetic and copies ran while one was open for 15% of the time, Pallas kernels for 0%

profile of v1, /device:TPU:1, one launch (start us, length us, event | category | flops | bytes accessed | tf_op | source)
XLA Modules:
  0.0 299.8 jit_solution(11170852844486399121)
XLA Ops:
  2.3 4.3 %fusion.16 = f32[137,32,128]{2,0,1:T(8,128)S(1)} fusion(f32[137,32,128]{2,1,0:T(8,128)S(1)} %copy-done, f32[137,137]{1,0:T(8,128)} %param.11), kind=kOutput, calls=%fused_computation.30 | convolution fusion | flops 922533888 | bytes 4564292 | tf_op jit(solution)/shard_map/kl,kxy->lxy/dot_general | solution.py:36
  6.6 3.9 %collective-permute-start.4 = (f32[137,1,128]{2,0,1:T(8,128)S(1)}, f32[137,1,128]{2,0,1:T(8,128)S(1)}, u32[]{:S(2)}, u32[]{:S(2)}) collective-permute-start(f32[137,1,128]{2,0,1:T(8,128)S(1)} %get-tuple-element.30), channel_id=1, source_target_pairs={{0,8},{8,16},{16,24},{24,32},{32,40},{40,48},{48,56},{56,64},{64,7... | collective-permute-start | bytes 210440 | tf_op jit(solution)/shard_map/ppermute | solution.py:29
  11.8 2.3 fusion.28
  14.2 4.0 %collective-permute-start = (bf16[137,5,1,128]{3,0,2,1:T(8,128)(2,1)S(1)}, bf16[137,5,1,128]{3,0,2,1:T(8,128)(2,1)S(1)}, u32[]{:S(2)}, u32[]{:S(2)}) collective-permute-start(bf16[137,5,1,128]{3,0,2,1:T(8,128)(2,1)S(1)} %copy.58), channel_id=1, source_target_pairs={{0,8},{8,16},{16,24},{24,32},{32,40},{40,48},{48,56},{56,64},{64,7... | collective-permute-start | bytes 526088 | tf_op jit(solution)/shard_map/ppermute | solution.py:29
  18.4 3.0 fusion.30
  21.4 3.0 copy.39
  24.4 4.6 %collective-permute-start.6 = (f32[137,34,1]{0,2,1:T(1,128)S(1)}, f32[137,34,1]{0,2,1:T(1,128)S(1)}, u32[]{:S(2)}, u32[]{:S(2)}) collective-permute-start(f32[137,34,1]{0,2,1:T(1,128)S(1)} %copy.39), channel_id=1, source_target_pairs={{0,1},{1,2},{2,3},{3,4},{4,5},{5,6},{6,7},{8,9},{9,10},{10,11},{11... | collective-permute-start | bytes 55904 | tf_op jit(solution)/shard_map/ppermute | solution.py:29
  29.0 3.0 copy.40
  37.5 2.3 copy.42
  39.9 5.2 %constant_dynamic-update-slice_fusion.1 = bf16[137,5,34,128]{3,0,2,1:T(8,128)(2,1)S(1)} fusion(bf16[137,5,34,128]{3,0,2,1:T(8,128)(2,1)S(1)} %constant_dynamic-update-slice_fusion.2, bf16[137,5,32,128]{3,2,1,0:T(8,128)(2,1)} %param.12), kind=kLoop, calls=%fused_computation.43 | loop fusion | bytes 11509760
  45.1 6.5 %fusion.27 = (bf16[137,5,34,1]{3,0,2,1:T(8,128)(2,1)}, bf16[137,5,34,1]{3,0,2,1:T(8,128)(2,1)}) fusion(bf16[137,5,34,128]{3,0,2,1:T(8,128)(2,1)S(1)} %constant_dynamic-update-slice_fusion), kind=kLoop, calls=%fused_computation.46 | loop fusion | bytes 186320 | tf_op jit(solution)/shard_map/slice | solution.py:27
  51.6 6.5 %copy.33 = bf16[137,5,34,1]{0,2,3,1:T(8,128)(2,1)S(1)} copy(bf16[137,5,34,1]{3,0,2,1:T(8,128)(2,1)} %get-tuple-element.20) | data formatting | bytes 93160 | tf_op jit(solution)/shard_map/slice | solution.py:27
  58.1 3.8 %collective-permute-start.2 = (bf16[137,5,34,1]{0,2,3,1:T(8,128)(2,1)S(1)}, bf16[137,5,34,1]{0,2,3,1:T(8,128)(2,1)S(1)}, u32[]{:S(2)}, u32[]{:S(2)}) collective-permute-start(bf16[137,5,34,1]{0,2,3,1:T(8,128)(2,1)S(1)} %copy.33), channel_id=1, source_target_pairs={{0,1},{1,2},{2,3},{3,4},{4,5},{5,6},{6,7},{8,9},{9,10},{10,11},{11... | collective-permute-start | bytes 139748 | tf_op jit(solution)/shard_map/ppermute | solution.py:29
  61.9 6.5 %copy.34 = bf16[137,5,34,1]{0,2,3,1:T(8,128)(2,1)S(1)} copy(bf16[137,5,34,1]{3,0,2,1:T(8,128)(2,1)} %get-tuple-element.21) | data formatting | bytes 93160 | tf_op jit(solution)/shard_map/slice | solution.py:28
  70.3 6.6 %pad_maximum_fusion = f32[137,34,130]{2,0,1:T(8,128)} fusion(f32[137,34,1]{2,0,1:T(8,128)} %copy.42, f32[137,1,128]{2,0,1:T(8,128)S(1)} %collective-permute-done.5, f32[137,32,128]{2,0,1:T(8,128)} %copy-done.14, f32[137,1,128]{2,0,1:T(8,128)S(1)} %collective-permute-done.4, f32[137,34,1]{2,0,1:T(8,128)} %copy.41), kind=kLoop, calls=%fused_computation.3 | loop fusion | flops 2422160 | bytes 4844320 | tf_op jit(solution)/shard_map/concatenate | solution.py:31
  76.9 4.8 %copy.35 = bf16[137,5,34,1]{3,0,2,1:T(8,128)(2,1)} copy(bf16[137,5,34,1]{0,2,3,1:T(8,128)(2,1)S(1)} %collective-permute-done.2) | data formatting | bytes 93160 | tf_op jit(solution)/shard_map/ppermute | solution.py:29
  81.7 4.9 %copy.36 = bf16[137,5,34,1]{3,0,2,1:T(8,128)(2,1)} copy(bf16[137,5,34,1]{0,2,3,1:T(8,128)(2,1)S(1)} %collective-permute-done.3) | data formatting | bytes 93160 | tf_op jit(solution)/shard_map/ppermute | solution.py:30
  86.6 14.5 %convert_bitcast_fusion.2 = (f32[137,34,130]{2,0,1:T(8,128)}, f32[137,34,130]{2,0,1:T(8,128)}, f32[137,34,130]{2,0,1:T(8,128)}, f32[137,34,130]{2,0,1:T(8,128)}) fusion(bf16[137,5,34,1]{3,0,2,1:T(8,128)(2,1)} %copy.36, bf16[137,5,34,128]{3,0,2,1:T(8,128)(2,1)} %copy-done.9, bf16[137,5,34,1]{3,0,2,1:T(8,128)(2,1)} %copy.35), kind=kLoop, calls=%fused_computation.2 | loop fusion | flops 14532960 | bytes 15744040 | tf_op jit(solution)/shard_map/squeeze | solution.py:42
  103.2 14.2 %fusion.22 = f32[137,32,128]{2,0,1:T(8,128)S(1)} fusion(f32[137,34,130]{2,0,1:T(8,128)} %pad_maximum_fusion, f32[137,32,128]{2,0,1:T(8,128)S(1)} %copy-done.15, bf16[137,1,32,128]{3,0,2,1:T(8,128)(2,1)S(1)} %pad_maximum_fusion.6, f32[137,34,130]{2,0,1:T(8,128)} %get-tuple-element.19, f32[137,34,130]{2,0,1:T(8,128)} %get-tuple-element.17, ...), kind=kOutput, calls=%fused_computation.36 | convolution fusion | flops 928145408 | bytes 24560964 | tf_op jit(solution)/shard_map/kl,kxy->lxy/dot_general | solution.py:36
  117.4 4.3 %collective-permute-start.8 = (f32[137,1,128]{2,0,1:T(8,128)S(1)}, f32[137,1,128]{2,0,1:T(8,128)S(1)}, u32[]{:S(2)}, u32[]{:S(2)}) collective-permute-start(f32[137,1,128]{2,0,1:T(8,128)S(1)} %get-tuple-element.28), channel_id=1, source_target_pairs={{0,8},{8,16},{16,24},{24,32},{32,40},{40,48},{48,56},{56,64},{64,7... | collective-permute-start | bytes 210440 | tf_op jit(solution)/shard_map/ppermute | solution.py:29
  123.1 3.7 %collective-permute-done.9 = f32[137,1,128]{2,0,1:T(8,128)S(1)} collective-permute-done((f32[137,1,128]{2,0,1:T(8,128)S(1)}, f32[137,1,128]{2,0,1:T(8,128)S(1)}, u32[]{:S(2)}, u32[]{:S(2)}) %collective-permute-start.9) | collective-permute-done | bytes 70176 | tf_op jit(solution)/shard_map/ppermute | solution.py:30
  127.0 3.1 %fusion.29 = (f32[137,34,1]{2,0,1:T(8,128)}, f32[137,34,1]{2,0,1:T(8,128)}) fusion(f32[137,34,128]{2,0,1:T(8,128)S(1)} %pad_maximum_fusion.5), kind=kLoop, calls=%fused_computation.48 | loop fusion | bytes 74528 | tf_op jit(solution)/shard_map/slice | solution.py:27
  130.1 3.0 %copy.44 = f32[137,34,1]{0,2,1:T(1,128)S(1)} copy(f32[137,34,1]{2,0,1:T(8,128)} %get-tuple-element.24) | data formatting | bytes 37264 | tf_op jit(solution)/shard_map/slice | solution.py:27
  133.1 5.3 %collective-permute-start.10 = (f32[137,34,1]{0,2,1:T(1,128)S(1)}, f32[137,34,1]{0,2,1:T(1,128)S(1)}, u32[]{:S(2)}, u32[]{:S(2)}) collective-permute-start(f32[137,34,1]{0,2,1:T(1,128)S(1)} %copy.44), channel_id=1, source_target_pairs={{0,1},{1,2},{2,3},{3,4},{4,5},{5,6},{6,7},{8,9},{9,10},{10,11},{11... | collective-permute-start | bytes 55904 | tf_op jit(solution)/shard_map/ppermute | solution.py:29
  138.4 3.0 copy.45
  144.0 2.3 copy.46
  146.6 2.3 copy.47
  149.0 5.3 %pad_maximum_fusion.1 = f32[137,34,130]{2,0,1:T(8,128)S(1)} fusion(f32[137,34,1]{2,0,1:T(8,128)} %copy.47, f32[137,1,128]{2,0,1:T(8,128)S(1)} %collective-permute-done.9, f32[137,32,128]{2,0,1:T(8,128)} %copy-done.12, f32[137,1,128]{2,0,1:T(8,128)S(1)} %collective-permute-done.8, f32[137,34,1]{2,0,1:T(8,128)} %copy.46), kind=kLoop, calls=%fused_computation.4 | loop fusion | flops 2422160 | bytes 4844320 | tf_op jit(solution)/shard_map/concatenate | solution.py:31
  154.2 8.0 %fusion = f32[137,32,128]{2,0,1:T(8,128)S(1)} fusion(f32[137,34,130]{2,0,1:T(8,128)S(1)} %pad_maximum_fusion.1, f32[137,32,128]{2,0,1:T(8,128)S(1)} %copy-done.13, bf16[137,1,32,128]{3,0,2,1:T(8,128)(2,1)S(1)} %pad_maximum_fusion.6, f32[137,34,130]{2,0,1:T(8,128)} %get-tuple-element.19, f32[137,34,130]{2,0,1:T(8,128)} %get-tuple-element.17, ...), kind=kLoop, calls=%fused_computation.11 | loop fusion | flops 5611520 | bytes 23568384 | tf_op jit(solution)/shard_map/add | solution.py:46
  163.0 78.8 %exchange.1.received = bf16[128,144,128]{2,1,0:T(8,128)(2,1)S(1)} custom-call(s32[16384]{0:T(1024)S(1)} %bitcast.43, f32[4384,128]{1,0:T(8,128)S(1)} %bitcast.41), custom_call_target="tpu_custom_call" | custom-call | tf_op jit(solution)/shard_map/exchange/pallas_call | solution.py:172
  243.9 39.3 %impacts.1 = (f32[64,128]{1,0:T(8,128)}, f32[32,128]{1,0:T(8,128)S(1)}) custom-call(s32[32768]{0:T(1024)S(1)} %bitcast.42, s32[1]{0:T(128)S(6)} %copy.62.valid, bf16[128,144,128]{2,1,0:T(8,128)(2,1)} %copy-done.2, bf16[137,8192]{1,0:T(8,128)(2,1)S(1)} %copy-done.4, f32[4,8192]{1,0:T(4,128)S(1)} %copy-done.5, f32[64,128]{1,0:T(8,128)S(1)} %bitcast.44, ...), custom_call_target="tpu_custom_call" | custom-call | tf_op jit(solution)/shard_map/impacts/pallas_call | solution.py:257
  283.8 14.8 %totals.1 = f32[8,128]{1,0:T(8,128)} custom-call(f32[32,128]{1,0:T(8,128)} %copy-done.8), custom_call_target="tpu_custom_call" | custom-call | tf_op jit(solution)/shard_map/totals/pallas_call | solution.py:321
  (69 shorter events, 21.2 us)
Async XLA Ops:
  0.6 1.6 copy-start
  6.5 11.7 %copy-start.14 = (f32[137,32,128]{2,0,1:T(8,128)}, f32[137,32,128]{2,0,1:T(8,128)S(1)}, u32[]{:S(2)}) copy-start(f32[137,32,128]{2,0,1:T(8,128)S(1)} %fusion.16) | copy-start | bytes 6733828
  6.6 11.6 %collective-permute-start.4 = (f32[137,1,128]{2,0,1:T(8,128)S(1)}, f32[137,1,128]{2,0,1:T(8,128)S(1)}, u32[]{:S(2)}, u32[]{:S(2)}) collective-permute-start(f32[137,1,128]{2,0,1:T(8,128)S(1)} %get-tuple-element.30), channel_id=1, source_target_pairs={{0,8},{8,16},{16,24},{24,32},{32,40},{40,48},{48,56},{56,64},{64,7... | collective-permute-start | bytes 210440 | tf_op jit(solution)/shard_map/ppermute | solution.py:29
  10.5 7.7 %collective-permute-start.5 = (f32[137,1,128]{2,0,1:T(8,128)S(1)}, f32[137,1,128]{2,0,1:T(8,128)S(1)}, u32[]{:S(2)}, u32[]{:S(2)}) collective-permute-start(f32[137,1,128]{2,0,1:T(8,128)S(1)} %get-tuple-element.31), channel_id=1, source_target_pairs={{8,0},{16,8},{24,16},{32,24},{40,32},{48,40},{56,48},{64,56},{72,6... | collective-permute-start | bytes 210440 | tf_op jit(solution)/shard_map/ppermute | solution.py:30
  14.2 25.6 %collective-permute-start = (bf16[137,5,1,128]{3,0,2,1:T(8,128)(2,1)S(1)}, bf16[137,5,1,128]{3,0,2,1:T(8,128)(2,1)S(1)}, u32[]{:S(2)}, u32[]{:S(2)}) collective-permute-start(bf16[137,5,1,128]{3,0,2,1:T(8,128)(2,1)S(1)} %copy.58), channel_id=1, source_target_pairs={{0,8},{8,16},{16,24},{24,32},{32,40},{40,48},{48,56},{56,64},{64,7... | collective-permute-start | bytes 526088 | tf_op jit(solution)/shard_map/ppermute | solution.py:29
  24.4 10.9 %collective-permute-start.6 = (f32[137,34,1]{0,2,1:T(1,128)S(1)}, f32[137,34,1]{0,2,1:T(1,128)S(1)}, u32[]{:S(2)}, u32[]{:S(2)}) collective-permute-start(f32[137,34,1]{0,2,1:T(1,128)S(1)} %copy.39), channel_id=1, source_target_pairs={{0,1},{1,2},{2,3},{3,4},{4,5},{5,6},{6,7},{8,9},{9,10},{10,11},{11... | collective-permute-start | bytes 55904 | tf_op jit(solution)/shard_map/ppermute | solution.py:29
  32.0 5.6 %collective-permute-start.7 = (f32[137,34,1]{0,2,1:T(1,128)S(1)}, f32[137,34,1]{0,2,1:T(1,128)S(1)}, u32[]{:S(2)}, u32[]{:S(2)}) collective-permute-start(f32[137,34,1]{0,2,1:T(1,128)S(1)} %copy.40), channel_id=1, source_target_pairs={{1,0},{2,1},{3,2},{4,3},{5,4},{6,5},{7,6},{9,8},{10,9},{11,10},{12... | collective-permute-start | bytes 55904 | tf_op jit(solution)/shard_map/ppermute | solution.py:30
  33.9 11.1 %collective-permute-start.1 = (bf16[137,5,1,128]{3,0,2,1:T(8,128)(2,1)S(1)}, bf16[137,5,1,128]{3,0,2,1:T(8,128)(2,1)S(1)}, u32[]{:S(2)}, u32[]{:S(2)}) collective-permute-start(bf16[137,5,1,128]{3,0,2,1:T(8,128)(2,1)S(1)} %copy.59), channel_id=1, source_target_pairs={{8,0},{16,8},{24,16},{32,24},{40,32},{48,40},{56,48},{64,56},{72,6... | collective-permute-start | bytes 526088 | tf_op jit(solution)/shard_map/ppermute | solution.py:30
  45.1 6.5 %copy-start.9 = (bf16[137,5,34,128]{3,0,2,1:T(8,128)(2,1)}, bf16[137,5,34,128]{3,0,2,1:T(8,128)(2,1)S(1)}, u32[]{:S(2)}) copy-start(bf16[137,5,34,128]{3,0,2,1:T(8,128)(2,1)S(1)} %constant_dynamic-update-slice_fusion) | copy-start | bytes 17886724
  58.1 18.8 %collective-permute-start.2 = (bf16[137,5,34,1]{0,2,3,1:T(8,128)(2,1)S(1)}, bf16[137,5,34,1]{0,2,3,1:T(8,128)(2,1)S(1)}, u32[]{:S(2)}, u32[]{:S(2)}) collective-permute-start(bf16[137,5,34,1]{0,2,3,1:T(8,128)(2,1)S(1)} %copy.33), channel_id=1, source_target_pairs={{0,1},{1,2},{2,3},{3,4},{4,5},{5,6},{6,7},{8,9},{9,10},{10,11},{11... | collective-permute-start | bytes 139748 | tf_op jit(solution)/shard_map/ppermute | solution.py:29
  68.4 13.3 %collective-permute-start.3 = (bf16[137,5,34,1]{0,2,3,1:T(8,128)(2,1)S(1)}, bf16[137,5,34,1]{0,2,3,1:T(8,128)(2,1)S(1)}, u32[]{:S(2)}, u32[]{:S(2)}) collective-permute-start(bf16[137,5,34,1]{0,2,3,1:T(8,128)(2,1)S(1)} %copy.34), channel_id=1, source_target_pairs={{1,0},{2,1},{3,2},{4,3},{5,4},{6,5},{7,6},{9,8},{10,9},{11,10},{12... | collective-permute-start | bytes 139748 | tf_op jit(solution)/shard_map/ppermute | solution.py:30
  86.6 14.5 %copy-start.10 = (bf16[137,5,34,1]{3,0,2,1:T(8,128)(2,1)S(1)}, bf16[137,5,34,1]{3,0,2,1:T(8,128)(2,1)}, u32[]{:S(2)}) copy-start(bf16[137,5,34,1]{3,0,2,1:T(8,128)(2,1)} %copy.35) | copy-start | bytes 139744
  86.6 14.5 %copy-start.11 = (bf16[137,5,34,1]{3,0,2,1:T(8,128)(2,1)S(1)}, bf16[137,5,34,1]{3,0,2,1:T(8,128)(2,1)}, u32[]{:S(2)}) copy-start(bf16[137,5,34,1]{3,0,2,1:T(8,128)(2,1)} %copy.36) | copy-start | bytes 139744
  101.1 2.0 copy-start.15
  101.1 2.0 copy-start.16
  103.2 19.8 %copy-start.18 = (s32[1,16384]{1,0:T(1,128)S(1)}, s32[1,16384]{1,0:T(1,128)}, u32[]{:S(2)}) copy-start(s32[1,16384]{1,0:T(1,128)} %param.14) | copy-start | bytes 196612
  117.4 9.6 %copy-start.12 = (f32[137,32,128]{2,0,1:T(8,128)}, f32[137,32,128]{2,0,1:T(8,128)S(1)}, u32[]{:S(2)}) copy-start(f32[137,32,128]{2,0,1:T(8,128)S(1)} %fusion.22) | copy-start | bytes 6733828
  117.4 5.7 %collective-permute-start.8 = (f32[137,1,128]{2,0,1:T(8,128)S(1)}, f32[137,1,128]{2,0,1:T(8,128)S(1)}, u32[]{:S(2)}, u32[]{:S(2)}) collective-permute-start(f32[137,1,128]{2,0,1:T(8,128)S(1)} %get-tuple-element.28), channel_id=1, source_target_pairs={{0,8},{8,16},{16,24},{24,32},{32,40},{40,48},{48,56},{56,64},{64,7... | collective-permute-start | bytes 210440 | tf_op jit(solution)/shard_map/ppermute | solution.py:29
  121.7 5.1 %collective-permute-start.9 = (f32[137,1,128]{2,0,1:T(8,128)S(1)}, f32[137,1,128]{2,0,1:T(8,128)S(1)}, u32[]{:S(2)}, u32[]{:S(2)}) collective-permute-start(f32[137,1,128]{2,0,1:T(8,128)S(1)} %get-tuple-element.29), channel_id=1, source_target_pairs={{8,0},{16,8},{24,16},{32,24},{40,32},{48,40},{56,48},{64,56},{72,6... | collective-permute-start | bytes 210440 | tf_op jit(solution)/shard_map/ppermute | solution.py:30
  130.1 13.2 %copy-start.17 = (s32[4,8192]{1,0:T(4,128)S(1)}, s32[4,8192]{1,0:T(4,128)}, u32[]{:S(2)}) copy-start(s32[4,8192]{1,0:T(4,128)} %param.15) | copy-start | bytes 393220
  133.1 10.9 %collective-permute-start.10 = (f32[137,34,1]{0,2,1:T(1,128)S(1)}, f32[137,34,1]{0,2,1:T(1,128)S(1)}, u32[]{:S(2)}, u32[]{:S(2)}) collective-permute-start(f32[137,34,1]{0,2,1:T(1,128)S(1)} %copy.44), channel_id=1, source_target_pairs={{0,1},{1,2},{2,3},{3,4},{4,5},{5,6},{6,7},{8,9},{9,10},{10,11},{11... | collective-permute-start | bytes 55904 | tf_op jit(solution)/shard_map/ppermute | solution.py:29
  141.4 5.3 %collective-permute-start.11 = (f32[137,34,1]{0,2,1:T(1,128)S(1)}, f32[137,34,1]{0,2,1:T(1,128)S(1)}, u32[]{:S(2)}, u32[]{:S(2)}) collective-permute-start(f32[137,34,1]{0,2,1:T(1,128)S(1)} %copy.45), channel_id=1, source_target_pairs={{1,0},{2,1},{3,2},{4,3},{5,4},{6,5},{7,6},{9,8},{10,9},{11,10},{12... | collective-permute-start | bytes 55904 | tf_op jit(solution)/shard_map/ppermute | solution.py:30
  149.0 5.3 %copy-start.13 = (f32[137,32,128]{2,0,1:T(8,128)S(1)}, f32[137,32,128]{2,0,1:T(8,128)}, u32[]{:S(2)}) copy-start(f32[137,32,128]{2,0,1:T(8,128)} %copy-done.12) | copy-start | bytes 6733828
  162.9 78.8 %copy-start.3 = (f32[137,32,128]{2,1,0:T(8,128)}, f32[137,32,128]{2,1,0:T(8,128)S(1)}, u32[]{:S(2)}) copy-start(f32[137,32,128]{2,1,0:T(8,128)S(1)} %copy.50) | copy-start | bytes 6733828
  163.0 81.0 %copy-start.4 = (bf16[137,8192]{1,0:T(8,128)(2,1)S(1)}, bf16[137,8192]{1,0:T(8,128)(2,1)}, u32[]{:S(2)}) copy-start(bf16[137,8192]{1,0:T(8,128)(2,1)} %jac.1) | copy-start | bytes 6733828
  163.0 81.0 %copy-start.5 = (f32[4,8192]{1,0:T(4,128)S(1)}, f32[4,8192]{1,0:T(4,128)}, u32[]{:S(2)}) copy-start(f32[4,8192]{1,0:T(4,128)} %weight.1) | copy-start | bytes 393220
  163.0 81.0 %copy-start.6 = (f32[8192]{0:T(1024)S(1)}, f32[8192]{0:T(1024)}, u32[]{:S(2)}) copy-start(f32[8192]{0:T(1024)} %param.18) | copy-start | bytes 98308
  163.0 81.0 %copy-start.7 = (s32[8192]{0:T(1024)S(1)}, s32[8192]{0:T(1024)}, u32[]{:S(2)}) copy-start(s32[8192]{0:T(1024)} %param.17) | copy-start | bytes 98308
  241.8 2.2 copy-start.2
  243.9 55.8 %copy-start.1 = (f32[137,32,128]{2,1,0:T(8,128)S(1)}, f32[137,32,128]{2,1,0:T(8,128)}, u32[]{:S(2)}) copy-start(f32[137,32,128]{2,1,0:T(8,128)} %param.10) | copy-start | bytes 6733828
  283.2 0.6 copy-start.8

commit v2 on v1

--- a/solution.py
+++ b/solution.py
@@ -19,46 +19,6 @@
 MIB = 1024 * 1024
 
 
-def padded_2(x, sides, width):
-    for axis, dim in sides:
-        size, length = (lax.axis_size(axis), x.shape[dim])
-        up = [(i, (i + 1) % size) for i in range(size - 1)]
-        down = [(j, i) for i, j in up]
-        last = lax.slice_in_dim(x, length - width, length, axis=dim)
-        leading = lax.slice_in_dim(x, 0, width, axis=dim)
-        before = lax.ppermute(last, axis, up)
-        after = lax.ppermute(leading, axis, down)
-        x = jnp.concatenate([before, x, after], axis=dim)
-    return x
-
-
-def vertical_mix(sensitivity, coupling):
-    return jnp.einsum("kl,kxy->lxy", coupling, sensitivity, precision=lax.Precision.HIGHEST)
-
-
-def spread(padded, coef_pad):
-    weights = coef_pad.astype(jnp.float32)
-    center = weights[..., 0, 1:-1, 1:-1] * padded[..., 1:-1, 1:-1]
-    east = (weights[..., 1, :, :] * padded)[..., :-2, 1:-1]
-    west = (weights[..., 2, :, :] * padded)[..., 2:, 1:-1]
-    north = (weights[..., 3, :, :] * padded)[..., 1:-1, :-2]
-    south = (weights[..., 4, :, :] * padded)[..., 1:-1, 2:]
-    return center + east + west + north + south
-
-
-def extend(sensitivity, rim_depth):
-    return padded_2(sensitivity, (("gx", 1), ("gy", 2)), rim_depth)
-
-
-def transport_steps(gradient, coupling, transport):
-    sensitivity = gradient
-    rim_depth = 1
-    coef_wide = padded_2(transport, (("gx", 2), ("gy", 3)), rim_depth)
-    for repeat in range(STEPS):
-        sensitivity = spread(extend(vertical_mix(sensitivity, coupling), 1), coef_wide)
-    return sensitivity
-
-
 def identity(rows, dtype):
     row = lax.broadcasted_iota(jnp.int32, (rows, LANES), 0)
     col = lax.broadcasted_iota(jnp.int32, (rows, LANES), 1)
@@ -79,9 +39,99 @@
     )
 
 
-def exchange_kernel(levels, columns, field, received, table, ga, gb, outgoing, send_sem, recv_sem, own_sem):
+def split(value):
+    high = value.astype(jnp.bfloat16)
+    return high, (value - high.astype(jnp.float32)).astype(jnp.bfloat16)
+
+
+def vertical_mix(levels, rows_x, coupling_t, source, mixed):
+    padded = coupling_t.shape[0]
+    stacked = jnp.concatenate(split(coupling_t[...]), axis=0)
+    pad = jnp.zeros((padded - levels, 2 * LANES), jnp.float32)
+
+    @pl.loop(0, rows_x // 2, unroll=2)
+    def _(t):
+        x = 2 * t
+        pair = jnp.concatenate(
+            [source[pl.ds(x, levels, stride=rows_x), :], source[pl.ds(x + 1, levels, stride=rows_x), :]], axis=1
+        )
+        high, low = split(jnp.concatenate([pair, pad], axis=0))
+        both = jnp.dot(stacked, high, preferred_element_type=jnp.float32)
+        out = both[:padded] + (
+            both[padded:] + jnp.dot(stacked[:padded], low, preferred_element_type=jnp.float32)
+        )
+        mixed[pl.ds(x, levels, stride=rows_x), :] = out[:levels, :LANES]
+        mixed[pl.ds(x + 1, levels, stride=rows_x), :] = out[:levels, LANES:]
+
+
+def spread(levels, rows_x, transport, mixed, out, row_edge, col_edge):
+    row = lax.broadcasted_iota(jnp.int32, (rows_x, LANES), 0)
+    lane = lax.broadcasted_iota(jnp.int32, (rows_x, LANES), 1)
+    col_edge[...] = jnp.zeros_like(col_edge)
+
+    @pl.loop(0, levels)
+    def _(l):
+        here = pl.ds(pl.multiple_of(l * rows_x, rows_x), rows_x)
+        u = mixed[here, :]
+        part = [transport[l, k].astype(jnp.float32) * u for k in range(5)]
+        down = pltpu.roll(part[1], 1, 0)
+        up = pltpu.roll(part[2], rows_x - 1, 0)
+        right = pltpu.roll(part[3], 1, 1)
+        left = pltpu.roll(part[4], LANES - 1, 1)
+        row_edge[0, pl.ds(l, 1), :] = down[0:1]
+        row_edge[1, pl.ds(l, 1), :] = up[rows_x - 1 : rows_x]
+        bank, spot = l // LANES, lax.rem(l, LANES)
+        at = lane == spot
+        col_edge[0, bank] = jnp.where(at, pltpu.roll(right, spot, 1), col_edge[0, bank])
+        col_edge[1, bank] = jnp.where(at, pltpu.roll(left, lax.rem(spot + 1, LANES), 1), col_edge[1, bank])
+        total = part[0] + jnp.where(row == 0, 0.0, down) + jnp.where(row == rows_x - 1, 0.0, up)
+        total = total + jnp.where(lane == 0, 0.0, right) + jnp.where(lane == LANES - 1, 0.0, left)
+        out[here, :] = total
+
+
+def add_edges(levels, rows_x, out, row_halo, col_halo, gx, gy, nx, ny):
+    lane = lax.broadcasted_iota(jnp.int32, (rows_x, LANES), 1)
+    first, last = pl.ds(0, levels, stride=rows_x), pl.ds(rows_x - 1, levels, stride=rows_x)
+    out[first, :] = out[first, :] + jnp.where(gx > 0, row_halo[0, 0:levels, :], 0.0)
+    out[last, :] = out[last, :] + jnp.where(gx < nx - 1, row_halo[1, 0:levels, :], 0.0)
+    at_first = (lane == 0) & (gy > 0)
+    at_last = (lane == LANES - 1) & (gy < ny - 1)
+
+    @pl.loop(0, levels)
+    def _(l):
+        here = pl.ds(pl.multiple_of(l * rows_x, rows_x), rows_x)
+        bank, spot = l // LANES, lax.rem(l, LANES)
+        before = pltpu.roll(col_halo[0, bank], lax.rem(LANES - spot, LANES), 1)
+        after = pltpu.roll(col_halo[1, bank], LANES - 1 - spot, 1)
+        out[here, :] = out[here, :] + jnp.where(at_first, before, 0.0) + jnp.where(at_last, after, 0.0)
+
+
+def exchange_kernel(
+    levels,
+    columns,
+    gradient,
+    coupling_t,
+    transport,
+    field,
+    received,
+    mixed,
+    row_edge,
+    col_edge,
+    row_halo,
+    col_halo,
+    table,
+    ga,
+    gb,
+    outgoing,
+    edge_send,
+    edge_recv,
+    send_sem,
+    recv_sem,
+    own_sem,
+):
     gx, gy = lax.axis_index("gx"), lax.axis_index("gy")
-    me = gx * 8 + gy
+    nx, ny = lax.axis_size("gx"), lax.axis_size("gy")
+    me = gx * ny + gy
     ranks = received.shape[0]
     barrier = pltpu.get_barrier_semaphore()
 
@@ -90,6 +140,34 @@
         pl.semaphore_signal(barrier, inc=1, device_id=peer(k), device_id_type=MESH)
 
     rows_x = field.shape[0] // levels
+    sides = (
+        (row_edge, row_halo, 0, (lax.rem(gx + 1, nx), gy)),
+        (row_edge, row_halo, 1, (lax.rem(gx + nx - 1, nx), gy)),
+        (col_edge, col_halo, 0, (gx, lax.rem(gy + 1, ny))),
+        (col_edge, col_halo, 1, (gx, lax.rem(gy + ny - 1, ny))),
+    )
+    for step in range(STEPS):
+        vertical_mix(levels, rows_x, coupling_t, gradient if step == 0 else field, mixed)
+        spread(levels, rows_x, transport, mixed, field, row_edge.at[step], col_edge.at[step])
+        if step == 0:
+            pl.semaphore_wait(barrier, ranks - 1)
+        copies = [
+            pltpu.make_async_remote_copy(
+                src_ref=edge.at[step, side],
+                dst_ref=halo.at[step, side],
+                send_sem=edge_send.at[step, i],
+                recv_sem=edge_recv.at[step, i],
+                device_id=device,
+                device_id_type=MESH,
+            )
+            for i, (edge, halo, side, device) in enumerate(sides)
+        ]
+        for copy in copies:
+            copy.start()
+        for copy in copies:
+            copy.wait()
+        add_edges(levels, rows_x, field, row_halo.at[step], col_halo.at[step], gx, gy, nx, ny)
+
     eye = identity(LANES, jnp.bfloat16)
 
     @pl.loop(0, rows_x, unroll=4)
@@ -101,20 +179,19 @@
         table[pl.ds(base + 1, LANES, stride=2), :] = dot_nt(eye, tail.astype(jnp.bfloat16))
 
     pick = identity(TAIL, jnp.bfloat16)
-    pl.semaphore_wait(barrier, ranks - 1)
 
     def step_at(k):
         return lax.rem((k + 1) * STRIDE, ranks)
 
     def owner_at(k):
         tx, ty = peer(step_at(k))
-        return tx * 8 + ty
+        return tx * ny + ty
 
     def copy_for(k):
         step = step_at(k)
         tx, ty = peer(step)
         return pltpu.make_async_remote_copy(
-            src_ref=outgoing.at[tx * 8 + ty],
+            src_ref=outgoing.at[tx * ny + ty],
             dst_ref=received.at[me],
             send_sem=send_sem.at[step],
             recv_sem=recv_sem.at[step],
@@ -161,31 +238,43 @@
     own.wait()
 
 
-def exchange(columns, field, ranks):
-    levels, rows_x, lanes = field.shape
-    flat = field.reshape(levels * rows_x, lanes)
+def exchange(columns, gradient, coupling, transport, ranks):
+    levels, rows_x, lanes = gradient.shape
+    flat = gradient.reshape(levels * rows_x, lanes)
+    padded = -(-levels // TAIL) * TAIL
+    coupling_t = jnp.pad(coupling.T, ((0, padded - levels), (0, padded - levels)))
     block = jax.ShapeDtypeStruct((ranks, BLOCK, LANES), jnp.bfloat16)
+    row_edges = pltpu.VMEM((STEPS, 2, padded, LANES), jnp.float32)
+    col_edges = pltpu.VMEM((STEPS, 2, 2, rows_x, LANES), jnp.float32)
 
     def kernel(*refs):
         exchange_kernel(levels, *refs)
 
-    return pl.pallas_call(
+    field, received = pl.pallas_call(
         kernel,
-        out_shape=block,
-        in_specs=[SMEM, VMEM],
-        out_specs=VMEM,
+        out_shape=(jax.ShapeDtypeStruct(flat.shape, jnp.float32), block),
+        in_specs=[SMEM, VMEM, VMEM, VMEM],
+        out_specs=(VMEM, VMEM),
         scratch_shapes=[
+            pltpu.VMEM(flat.shape, jnp.float32),
+            row_edges,
+            col_edges,
+            row_edges,
+            col_edges,
             pltpu.VMEM((rows_x * lanes * 2, LANES), jnp.float32),
             pltpu.VMEM((2 * LANES, LANES), jnp.float32),
             pltpu.VMEM((2 * LANES, LANES), jnp.float32),
             pltpu.VMEM(block.shape, block.dtype),
+            pltpu.SemaphoreType.DMA((STEPS, 4)),
+            pltpu.SemaphoreType.DMA((STEPS, 4)),
             pltpu.SemaphoreType.DMA((ranks,)),
             pltpu.SemaphoreType.DMA((ranks,)),
             pltpu.SemaphoreType.DMA,
         ],
-        compiler_params=pltpu.CompilerParams(collective_id=1, has_side_effects=True, vmem_limit_bytes=40 * MIB),
+        compiler_params=pltpu.CompilerParams(collective_id=1, has_side_effects=True, vmem_limit_bytes=48 * MIB),
         name="exchange",
-    )(columns, flat)
+    )(columns, flat, coupling_t, transport)
+    return field.reshape(gradient.shape), received
 
 
 def impact_kernel(slots, valid, received, jac, weight, innovation, inst, impact, part, table, ga, gb):
@@ -348,9 +437,8 @@
     valid_count,
 ):
     nx, ny = lax.axis_size("gx"), lax.axis_size("gy")
-    sensitivity = transport_steps(gradient, coupling, transport)
     columns = jnp.maximum(send_cols[0], 0) * 2
-    received = exchange(columns, sensitivity, nx * ny)
+    sensitivity, received = exchange(columns, gradient, coupling, transport, nx * ny)
     impact, part = impacts(
         obs_slots, valid_count, received, obs_jacobian, obs_weight, innovation, obs_inst
     )

time: 301 us -> 216 us (0.72)
  Pallas kernels: 133 us -> 207 us
  local copies, waits for them, and re-layouts: 70.4 us -> 5.84 us
  other arithmetic: 36.7 us -> 0.96 us
  starting transfers between devices: 35.6 us -> 0 us
  matrix products: 18.5 us -> 0 us
  waiting for transfers between devices: 4 us -> 0 us
    pallas_call x1, Pallas kernels: 78.8 us -> 154 us  [exchange(): pl.pallas_call(kernel, out_shape=(jax.ShapeDtypeStruct(flat.shape, jnp.fl...]
    slice x12 -> x0, local copies, waits for them, and re-layouts: 39.8 us -> none  [the longest x8 25.1 us: padded_2(): last = lax.slice_in_dim(x, length - width, length, axis=dim)]
    ppermute x12 -> x0, starting transfers between devices: 35.6 us -> none  [the longest x6 25.9 us: padded_2(): before = lax.ppermute(last, axis, up)]
    ppermute x6 -> x0, local copies, waits for them, and re-layouts: 19 us -> none  [the longest x3 9.52 us: padded_2(): after = lax.ppermute(leading, axis, down)]
    dot_general x2 -> x0, matrix products: 18.5 us -> none  [vertical_mix(): jnp.einsum('kl,kxy->lxy', coupling, sensitivity, precision=lax.Precision....]
    squeeze x1 -> x0, other arithmetic: 14.5 us -> none  [spread(): east = (weights[..., 1, :, :] * padded)[..., :-2, 1:-1]]
    concatenate x4 -> x0, other arithmetic: 12.2 us -> none  [padded_2(): x = jnp.concatenate([before, x, after], axis=dim)]
    add x1 -> x0, other arithmetic: 7.97 us -> none  [spread(): return center + east + west + north + south]
  transfers between devices with their start and end apart: 12 -> 0, of which waited for: 2 -> 0; matrix products, arithmetic and copies ran while one was open for 15% -> 0% of each run, Pallas kernels for 0% -> 0%
where the time goes in v2:
time: 216 us
  Pallas kernels  207 us (96%)
  local copies, waits for them, and re-layouts  5.84 us (3%)
    pallas_call x1, Pallas kernels, exchange(): pl.pallas_call(kernel, out_shape=(jax.ShapeDtypeStruct(flat.shape, jnp.fl...  154 us
    pallas_call x1, Pallas kernels, impacts(): pl.pallas_call(impact_kernel, out_shape=(jax.ShapeDtypeStruct((chunks, LA...  39.3 us
    pallas_call x1, Pallas kernels, instrument_totals(): pl.pallas_call(total_kernel, out_shape=jax.ShapeDtypeStruct((8, LANES), j...  13.7 us
    unnamed x16, local copies, waits for them, and re-layouts  4.63 us

profile of v2, /device:TPU:1, one launch (start us, length us, event | category | flops | bytes accessed | tf_op | source)
XLA Modules:
  0.0 215.6 jit_solution(13287649734119626714)
XLA Ops:
  0.6 1.0 copy.14
  1.7 0.9 maximum_multiply_fusion
  2.6 0.0 copy-start.1
  2.6 1.6 copy-done.1
  4.2 0.0 copy-start.6
  4.2 0.0 copy-start
  4.2 0.0 copy-start.2
  4.2 0.0 copy-start.3
  4.2 0.0 copy-start.4
  4.3 154.5 %exchange.1 = (f32[4384,128]{1,0:T(8,128)S(1)}, bf16[128,144,128]{2,1,0:T(8,128)(2,1)}) custom-call(s32[16384]{0:T(1024)S(1)} %bitcast.17, f32[4384,128]{1,0:T(8,128)S(1)} %bitcast.14, f32[144,144]{1,0:T(8,128)S(1)} %pad.4.refs_2_, bf16[137,5,32,128]{3,2,1,0:T(8,128)(2,1)} %refs_3_.1), custom_call_target="tpu_custom_call" | custom-call | tf_op jit(solution)/shard_map/exchange/pallas_call | solution.py:253
  158.7 0.0 copy-done.6
  159.4 0.0 copy-done
  159.4 0.0 copy-done.2
  159.4 0.0 copy-done.3
  159.4 0.0 copy-done.4
  159.5 39.3 %impacts.1 = (f32[64,128]{1,0:T(8,128)}, f32[32,128]{1,0:T(8,128)S(1)}) custom-call(s32[32768]{0:T(1024)S(1)} %bitcast.16, s32[1]{0:T(128)S(6)} %copy.17.valid, bf16[128,144,128]{2,1,0:T(8,128)(2,1)} %get-tuple-element.8.received, bf16[137,8192]{1,0:T(8,128)(2,1)S(1)} %copy-done, f32[4,8192]{1,0:T(4,128)S(1)} %copy-done.2, f32[64,128]{1,0:T(8,128)S(1)} %bitcast.18, ...), custom_call_target="tpu_custom_call" | custom-call | tf_op jit(solution)/shard_map/impacts/pallas_call | solution.py:346
  198.7 0.0 copy-start.5
  198.7 0.6 copy-done.5
  199.3 13.7 %totals.1 = f32[8,128]{1,0:T(8,128)} custom-call(f32[32,128]{1,0:T(8,128)} %copy-done.5), custom_call_target="tpu_custom_call" | custom-call | tf_op jit(solution)/shard_map/totals/pallas_call | solution.py:410
  213.1 1.2 slice_bitcast_fusion
  214.3 1.4 copy.18
  (2 shorter events, 0.0 us)
Async XLA Ops:
  2.6 1.6 copy-start.1
  4.2 154.5 %copy-start.6 = (s32[4,8192]{1,0:T(4,128)S(1)}, s32[4,8192]{1,0:T(4,128)}, u32[]{:S(2)}) copy-start(s32[4,8192]{1,0:T(4,128)} %param.15) | copy-start | bytes 393220
  4.2 155.2 %copy-start = (bf16[137,8192]{1,0:T(8,128)(2,1)S(1)}, bf16[137,8192]{1,0:T(8,128)(2,1)}, u32[]{:S(2)}) copy-start(bf16[137,8192]{1,0:T(8,128)(2,1)} %jac.1) | copy-start | bytes 6733828
  4.2 155.2 %copy-start.2 = (f32[4,8192]{1,0:T(4,128)S(1)}, f32[4,8192]{1,0:T(4,128)}, u32[]{:S(2)}) copy-start(f32[4,8192]{1,0:T(4,128)} %weight.1) | copy-start | bytes 393220
  4.2 155.2 %copy-start.3 = (f32[8192]{0:T(1024)S(1)}, f32[8192]{0:T(1024)}, u32[]{:S(2)}) copy-start(f32[8192]{0:T(1024)} %param.18) | copy-start | bytes 98308
  4.2 155.2 %copy-start.4 = (s32[8192]{0:T(1024)S(1)}, s32[8192]{0:T(1024)}, u32[]{:S(2)}) copy-start(s32[8192]{0:T(1024)} %param.17) | copy-start | bytes 98308
  198.7 0.6 copy-start.5

commit v3 on v2

--- a/solution.py
+++ b/solution.py
@@ -12,6 +12,7 @@
 TAIL = 16
 BLOCK = MAIN + TAIL
 GROUP = 8
+WIDE = 8
 STRIDE = 37
 MESH = pl.DeviceIdType.MESH
 VMEM = pl.BlockSpec(memory_space=pltpu.VMEM)
@@ -64,29 +65,48 @@
         mixed[pl.ds(x + 1, levels, stride=rows_x), :] = out[:levels, LANES:]
 
 
+def by_bank(levels, work):
+    for bank, first in enumerate(range(0, levels, LANES)):
+        count = min(LANES, levels - first)
+        whole = count // WIDE
+
+        @pl.loop(0, whole)
+        def _(t):
+            work(bank, first, t * WIDE, WIDE)
+
+        if count % WIDE:
+            work(bank, first, whole * WIDE, count % WIDE)
+
+
 def spread(levels, rows_x, transport, mixed, out, row_edge, col_edge):
     row = lax.broadcasted_iota(jnp.int32, (rows_x, LANES), 0)
     lane = lax.broadcasted_iota(jnp.int32, (rows_x, LANES), 1)
     col_edge[...] = jnp.zeros_like(col_edge)
 
-    @pl.loop(0, levels)
-    def _(l):
-        here = pl.ds(pl.multiple_of(l * rows_x, rows_x), rows_x)
-        u = mixed[here, :]
-        part = [transport[l, k].astype(jnp.float32) * u for k in range(5)]
-        down = pltpu.roll(part[1], 1, 0)
-        up = pltpu.roll(part[2], rows_x - 1, 0)
-        right = pltpu.roll(part[3], 1, 1)
-        left = pltpu.roll(part[4], LANES - 1, 1)
-        row_edge[0, pl.ds(l, 1), :] = down[0:1]
-        row_edge[1, pl.ds(l, 1), :] = up[rows_x - 1 : rows_x]
-        bank, spot = l // LANES, lax.rem(l, LANES)
-        at = lane == spot
-        col_edge[0, bank] = jnp.where(at, pltpu.roll(right, spot, 1), col_edge[0, bank])
-        col_edge[1, bank] = jnp.where(at, pltpu.roll(left, lax.rem(spot + 1, LANES), 1), col_edge[1, bank])
-        total = part[0] + jnp.where(row == 0, 0.0, down) + jnp.where(row == rows_x - 1, 0.0, up)
-        total = total + jnp.where(lane == 0, 0.0, right) + jnp.where(lane == LANES - 1, 0.0, left)
-        out[here, :] = total
+    def work(bank, first, spot, width):
+        right_edge, left_edge = col_edge[0, bank], col_edge[1, bank]
+        for i in range(width):
+            at = spot + i
+            l = first + at
+            here = pl.ds(pl.multiple_of(l * rows_x, rows_x), rows_x)
+            u = mixed[here, :]
+            part = [transport[l, k].astype(jnp.float32) * u for k in range(5)]
+            down = pltpu.roll(part[1], 1, 0)
+            up = pltpu.roll(part[2], rows_x - 1, 0)
+            right = pltpu.roll(part[3], 1, 1)
+            left = pltpu.roll(part[4], LANES - 1, 1)
+            row_edge[0, pl.ds(l, 1), :] = down[0:1]
+            row_edge[1, pl.ds(l, 1), :] = up[rows_x - 1 : rows_x]
+            mine = lane == at
+            right_edge = jnp.where(mine, pltpu.roll(part[3], lax.rem(at + 1, LANES), 1), right_edge)
+            left_edge = jnp.where(mine, pltpu.roll(part[4], at, 1), left_edge)
+            total = part[0] + jnp.where(row == 0, 0.0, down) + jnp.where(row == rows_x - 1, 0.0, up)
+            total = total + jnp.where(lane == 0, 0.0, right) + jnp.where(lane == LANES - 1, 0.0, left)
+            out[here, :] = total
+        col_edge[0, bank] = right_edge
+        col_edge[1, bank] = left_edge
+
+    by_bank(levels, work)
 
 
 def add_edges(levels, rows_x, out, row_halo, col_halo, gx, gy, nx, ny):
@@ -97,13 +117,28 @@
     at_first = (lane == 0) & (gy > 0)
     at_last = (lane == LANES - 1) & (gy < ny - 1)
 
-    @pl.loop(0, levels)
-    def _(l):
-        here = pl.ds(pl.multiple_of(l * rows_x, rows_x), rows_x)
-        bank, spot = l // LANES, lax.rem(l, LANES)
-        before = pltpu.roll(col_halo[0, bank], lax.rem(LANES - spot, LANES), 1)
-        after = pltpu.roll(col_halo[1, bank], LANES - 1 - spot, 1)
-        out[here, :] = out[here, :] + jnp.where(at_first, before, 0.0) + jnp.where(at_last, after, 0.0)
+    def work(bank, start, spot, width):
+        before_all, after_all = col_halo[0, bank], col_halo[1, bank]
+        for i in range(width):
+            at = spot + i
+            here = pl.ds(pl.multiple_of((start + at) * rows_x, rows_x), rows_x)
+            before = pltpu.roll(before_all, lax.rem(LANES - at, LANES), 1)
+            after = pltpu.roll(after_all, LANES - 1 - at, 1)
+            out[here, :] = out[here, :] + jnp.where(at_first, before, jnp.where(at_last, after, 0.0))
+
+    by_bank(levels, work)
+
+
+def build_table(levels, rows_x, field, table):
+    eye = identity(LANES, jnp.bfloat16)
+
+    @pl.loop(0, rows_x, unroll=4)
+    def _(x):
+        slab = field[pl.ds(x, levels, stride=rows_x), :]
+        tail = jnp.concatenate([slab[MAIN:levels], jnp.zeros((2 * MAIN - levels, LANES), jnp.float32)], axis=0)
+        base = pl.multiple_of(x * 2 * LANES, 2 * LANES)
+        table[pl.ds(base, LANES, stride=2), :] = dot_nt(eye, slab[:MAIN].astype(jnp.bfloat16))
+        table[pl.ds(base + 1, LANES, stride=2), :] = dot_nt(eye, tail.astype(jnp.bfloat16))
 
 
 def exchange_kernel(
@@ -168,16 +203,7 @@
             copy.wait()
         add_edges(levels, rows_x, field, row_halo.at[step], col_halo.at[step], gx, gy, nx, ny)
 
-    eye = identity(LANES, jnp.bfloat16)
-
-    @pl.loop(0, rows_x, unroll=4)
-    def _(x):
-        slab = field[pl.ds(x, levels, stride=rows_x), :]
-        tail = jnp.concatenate([slab[MAIN:levels], jnp.zeros((2 * MAIN - levels, LANES), jnp.float32)], axis=0)
-        base = pl.multiple_of(x * 2 * LANES, 2 * LANES)
-        table[pl.ds(base, LANES, stride=2), :] = dot_nt(eye, slab[:MAIN].astype(jnp.bfloat16))
-        table[pl.ds(base + 1, LANES, stride=2), :] = dot_nt(eye, tail.astype(jnp.bfloat16))
-
+    build_table(levels, rows_x, field, table)
     pick = identity(TAIL, jnp.bfloat16)
 
     def step_at(k):

time: 216 us -> 166 us (0.77)
  Pallas kernels: 207 us -> 157 us
    pallas_call x1, Pallas kernels: 154 us -> 104 us  [exchange(): pl.pallas_call(kernel, out_shape=(jax.ShapeDtypeStruct(flat.shape, jnp.fl...]
where the time goes in v3:
time: 166 us; the launch traced here: 165 us
  Pallas kernels  157 us (95%)
  local copies, waits for them, and re-layouts  5.84 us (4%)
    pallas_call x1, Pallas kernels, exchange(): pl.pallas_call(kernel, out_shape=(jax.ShapeDtypeStruct(flat.shape, jnp.fl...  104 us
    pallas_call x1, Pallas kernels, impacts(): pl.pallas_call(impact_kernel, out_shape=(jax.ShapeDtypeStruct((chunks, LA...  39.3 us
    pallas_call x1, Pallas kernels, instrument_totals(): pl.pallas_call(total_kernel, out_shape=jax.ShapeDtypeStruct((8, LANES), j...  13.7 us
    unnamed x16, local copies, waits for them, and re-layouts  4.63 us

profile of v3, /device:TPU:1, one launch (start us, length us, event | category | flops | bytes accessed | tf_op | source)
XLA Modules:
  0.0 165.4 jit_solution(7666376664113200193)
XLA Ops:
  0.6 1.0 copy.14
  1.7 0.9 maximum_multiply_fusion
  2.6 0.0 copy-start.1
  2.6 1.6 copy-done.1
  4.2 0.0 copy-start.6
  4.2 0.0 copy-start
  4.2 0.0 copy-start.2
  4.2 0.0 copy-start.3
  4.2 0.0 copy-start.4
  4.3 104.2 %exchange.1 = (f32[4384,128]{1,0:T(8,128)S(1)}, bf16[128,144,128]{2,1,0:T(8,128)(2,1)}) custom-call(s32[16384]{0:T(1024)S(1)} %bitcast.17, f32[4384,128]{1,0:T(8,128)S(1)} %bitcast.14, f32[144,144]{1,0:T(8,128)S(1)} %pad.4.refs_2_, bf16[137,5,32,128]{3,2,1,0:T(8,128)(2,1)} %refs_3_.1), custom_call_target="tpu_custom_call" | custom-call | tf_op jit(solution)/shard_map/exchange/pallas_call | solution.py:279
  108.5 0.0 copy-done.6
  109.2 0.0 copy-done
  109.2 0.0 copy-done.2
  109.2 0.0 copy-done.3
  109.2 0.0 copy-done.4
  109.2 39.3 %impacts.1 = (f32[64,128]{1,0:T(8,128)}, f32[32,128]{1,0:T(8,128)S(1)}) custom-call(s32[32768]{0:T(1024)S(1)} %bitcast.16, s32[1]{0:T(128)S(6)} %copy.17.valid, bf16[128,144,128]{2,1,0:T(8,128)(2,1)} %get-tuple-element.8.received, bf16[137,8192]{1,0:T(8,128)(2,1)S(1)} %copy-done, f32[4,8192]{1,0:T(4,128)S(1)} %copy-done.2, f32[64,128]{1,0:T(8,128)S(1)} %bitcast.18, ...), custom_call_target="tpu_custom_call" | custom-call | tf_op jit(solution)/shard_map/impacts/pallas_call | solution.py:372
  148.5 0.0 copy-start.5
  148.5 0.6 copy-done.5
  149.1 13.7 %totals.1 = f32[8,128]{1,0:T(8,128)} custom-call(f32[32,128]{1,0:T(8,128)} %copy-done.5), custom_call_target="tpu_custom_call" | custom-call | tf_op jit(solution)/shard_map/totals/pallas_call | solution.py:436
  162.9 1.2 slice_bitcast_fusion
  164.1 1.4 copy.18
  (2 shorter events, 0.0 us)
Async XLA Ops:
  2.6 1.6 copy-start.1
  4.2 104.3 %copy-start.6 = (s32[4,8192]{1,0:T(4,128)S(1)}, s32[4,8192]{1,0:T(4,128)}, u32[]{:S(2)}) copy-start(s32[4,8192]{1,0:T(4,128)} %param.15) | copy-start | bytes 393220
  4.2 105.0 %copy-start = (bf16[137,8192]{1,0:T(8,128)(2,1)S(1)}, bf16[137,8192]{1,0:T(8,128)(2,1)}, u32[]{:S(2)}) copy-start(bf16[137,8192]{1,0:T(8,128)(2,1)} %jac.1) | copy-start | bytes 6733828
  4.2 105.0 %copy-start.2 = (f32[4,8192]{1,0:T(4,128)S(1)}, f32[4,8192]{1,0:T(4,128)}, u32[]{:S(2)}) copy-start(f32[4,8192]{1,0:T(4,128)} %weight.1) | copy-start | bytes 393220
  4.2 105.0 %copy-start.3 = (f32[8192]{0:T(1024)S(1)}, f32[8192]{0:T(1024)}, u32[]{:S(2)}) copy-start(f32[8192]{0:T(1024)} %param.18) | copy-start | bytes 98308
  4.2 105.0 %copy-start.4 = (s32[8192]{0:T(1024)S(1)}, s32[8192]{0:T(1024)}, u32[]{:S(2)}) copy-start(s32[8192]{0:T(1024)} %param.17) | copy-start | bytes 98308
  148.5 0.6 copy-start.5

commit v4 on v3

v4 whole, which is shorter than its diff:
```python
import jax
import jax.numpy as jnp
from jax import lax
from jax.experimental import pallas as pl
from jax.experimental.pallas import tpu as pltpu
from jax.sharding import PartitionSpec as P

NI = 32
STEPS = 2
LANES = 128
MAIN = 128
TAIL = 16
BLOCK = MAIN + TAIL
GROUP = 8
WIDE = 8
MIX_UNROLL = 2
FRONT = 8
POINTS = 4
EXPAND = 4
STRIDE = 37
MESH = pl.DeviceIdType.MESH
VMEM = pl.BlockSpec(memory_space=pltpu.VMEM)
SMEM = pl.BlockSpec(memory_space=pltpu.SMEM)
ANY = pl.BlockSpec(memory_space=pl.ANY)
MIB = 1024 * 1024


def identity(rows, dtype):
    row = lax.broadcasted_iota(jnp.int32, (rows, LANES), 0)
    col = lax.broadcasted_iota(jnp.int32, (rows, LANES), 1)
    return (row == col).astype(dtype)


def dot_nt(a, b):
    return lax.dot_general(a, b, (((1,), (1,)), ((), ())), preferred_element_type=jnp.float32)


def moved(step, sign):
    gx, gy = lax.axis_index("gx"), lax.axis_index("gy")
    z, x, y, core = gx // 4, lax.rem(gx, 4), gy // 2, lax.rem(gy, 2)
    dz, dx, dy, dc = lax.rem(step, 4), lax.rem(step // 4, 4), lax.rem(step // 16, 4), step // 64
    if sign < 0:
        dz, dx, dy = 4 - dz, 4 - dx, 4 - dy
    return (
        lax.rem(z + dz, 4) * 4 + lax.rem(x + dx, 4),
        lax.rem(y + dy, 4) * 2 + lax.rem(core + dc, 2),
    )


def peer(step):
    return moved(step, 1)


def split(value):
    high = value.astype(jnp.bfloat16)
    return high, (value - high.astype(jnp.float32)).astype(jnp.bfloat16)


def product(parts_a, parts_b):
    high_a, low_a = parts_a
    high_b, low_b = parts_b
    one = jnp.dot(high_a, high_b, preferred_element_type=jnp.float32)
    two = jnp.dot(low_a, high_b, preferred_element_type=jnp.float32)
    return one + (two + jnp.dot(high_a, low_b, preferred_element_type=jnp.float32))


def vertical_mix(levels, rows_x, coupling_t, source, mixed):
    padded = coupling_t.shape[1]
    stacked = coupling_t[...].reshape(2 * padded, padded)
    pad = jnp.zeros((padded - levels, 2 * LANES), jnp.float32)

    @pl.loop(0, rows_x // 2, unroll=MIX_UNROLL)
    def _(t):
        x = 2 * t
        pair = jnp.concatenate(
            [source[pl.ds(x, levels, stride=rows_x), :], source[pl.ds(x + 1, levels, stride=rows_x), :]], axis=1
        )
        high, low = split(jnp.concatenate([pair, pad], axis=0))
        both = jnp.dot(stacked, high, preferred_element_type=jnp.float32)
        out = both[:padded] + (
            both[padded:] + jnp.dot(stacked[:padded], low, preferred_element_type=jnp.float32)
        )
        mixed[pl.ds(x, levels, stride=rows_x), :] = out[:levels, :LANES]
        mixed[pl.ds(x + 1, levels, stride=rows_x), :] = out[:levels, LANES:]


def by_bank(levels, work):
    for bank, first in enumerate(range(0, levels, LANES)):
        count = min(LANES, levels - first)
        whole = count // WIDE

        @pl.loop(0, whole)
        def _(t):
            work(bank, first, t * WIDE, WIDE)

        if count % WIDE:
            work(bank, first, whole * WIDE, count % WIDE)


def at_edges(lane, first, last):
    return jnp.where(lane == 0, first, jnp.where(lane == LANES - 1, last, 0.0))


def spread(levels, rows_x, transport, mixed, out, row_edge, col_edge, col_mixed, col_own):
    row = lax.broadcasted_iota(jnp.int32, (rows_x, LANES), 0)
    lane = lax.broadcasted_iota(jnp.int32, (rows_x, LANES), 1)

    def work(bank, first, spot, width):
        right_edge, left_edge = col_edge[0, bank], col_edge[1, bank]
        if col_mixed is not None:
            before_all, after_all = col_mixed[0, bank], col_mixed[1, bank]
            first_own, last_own = col_own[0, bank], col_own[1, bank]
        for i in range(width):
            at = spot + i
            l = first + at
            here = pl.ds(pl.multiple_of(l * rows_x, rows_x), rows_x)
            u = mixed[here, :]
            if col_mixed is not None:
                before = pltpu.roll(before_all, lax.rem(LANES - at, LANES), 1)
                after = pltpu.roll(after_all, LANES - 1 - at, 1)
                u = u + at_edges(lane, before, after)
            part = [transport[l, k].astype(jnp.float32) * u for k in range(5)]
            down = pltpu.roll(part[1], 1, 0)
            up = pltpu.roll(part[2], rows_x - 1, 0)
            right = pltpu.roll(part[3], 1, 1)
            left = pltpu.roll(part[4], LANES - 1, 1)
            row_edge[0, pl.ds(l, 1), :] = down[0:1]
            row_edge[1, pl.ds(l, 1), :] = up[rows_x - 1 : rows_x]
            mine = lane == at
            right_edge = jnp.where(mine, pltpu.roll(part[3], lax.rem(at + 1, LANES), 1), right_edge)
            left_edge = jnp.where(mine, pltpu.roll(part[4], at, 1), left_edge)
            total = part[0] + jnp.where(row == 0, 0.0, down) + jnp.where(row == rows_x - 1, 0.0, up)
            total = total + jnp.where(lane == 0, 0.0, right) + jnp.where(lane == LANES - 1, 0.0, left)
            out[here, :] = total
            if col_mixed is not None:
                first_own = jnp.where(mine, pltpu.roll(total, at, 1), first_own)
                last_own = jnp.where(mine, pltpu.roll(total, lax.rem(at + 1, LANES), 1), last_own)
        col_edge[0, bank] = right_edge
        col_edge[1, bank] = left_edge
        if col_mixed is not None:
            col_own[0, bank] = first_own
            col_own[1, bank] = last_own

    by_bank(levels, work)


def add_columns(levels, rows_x, out, col_halo):
    lane = lax.broadcasted_iota(jnp.int32, (rows_x, LANES), 1)

    def work(bank, start, spot, width):
        before_all, after_all = col_halo[0, bank], col_halo[1, bank]
        for i in range(width):
            at = spot + i
            here = pl.ds(pl.multiple_of((start + at) * rows_x, rows_x), rows_x)
            before = pltpu.roll(before_all, lax.rem(LANES - at, LANES), 1)
            after = pltpu.roll(after_all, LANES - 1 - at, 1)
            out[here, :] = out[here, :] + at_edges(lane, before, after)

    by_bank(levels, work)


def table_rows(levels, rows_x, field, table, x):
    eye = identity(LANES, jnp.bfloat16)
    slab = field[pl.ds(x, levels, stride=rows_x), :]
    tail = jnp.concatenate([slab[MAIN:levels], jnp.zeros((2 * MAIN - levels, LANES), jnp.float32)], axis=0)
    base = FRONT + x * 2 * LANES
    table[pl.ds(base, LANES, stride=2), :] = dot_nt(eye, slab[:MAIN].astype(jnp.bfloat16))
    table[pl.ds(base + 1, LANES, stride=2), :] = dot_nt(eye, tail.astype(jnp.bfloat16))


def whole_kernel(
    columns,
    valid,
    gradient,
    coupling,
    transport_in,
    jac_in,
    slots_in,
    weight,
    innovation,
    inst,
    field,
    impact,
    total,
    transport,
    jac,
    slots_v,
    slots,
    square,
    coupling_t,
    mixed,
    row_edge,
    col_edge,
    row_halo,
    col_halo,
    col_mixed,
    col_own,
    table,
    ga,
    gb,
    outgoing,
    received,
    profiles,
    oa,
    ob,
    part,
    shares,
    edge_send,
    edge_recv,
    send_sem,
    recv_sem,
    share_send,
    share_recv,
    local_sem,
):
    gx, gy = lax.axis_index("gx"), lax.axis_index("gy")
    nx, ny = lax.axis_size("gx"), lax.axis_size("gy")
    me = gx * ny + gy
    ranks = received.shape[0]
    levels = coupling.shape[0]
    rows_x = field.shape[0] // levels
    padded = coupling_t.shape[1]
    chunks = impact.shape[0]
    barrier = pltpu.get_barrier_semaphore()

    load_transport = pltpu.make_async_copy(transport_in, transport, local_sem.at[0])
    load_transport.start()
    load_jac = pltpu.make_async_copy(jac_in, jac, local_sem.at[1])
    load_jac.start()

    @pl.loop(1, ranks)
    def _(k):
        pl.semaphore_signal(barrier, inc=1, device_id=peer(k), device_id_type=MESH)

    square[...] = jnp.zeros_like(square)
    square[0:levels, 0:levels] = coupling[...]
    coupling_parts = split(square[...])
    side = square.shape[0]
    wide_eye = (
        lax.broadcasted_iota(jnp.int32, (padded, side), 0) == lax.broadcasted_iota(jnp.int32, (padded, side), 1)
    ).astype(jnp.bfloat16)
    for i in range(2):
        coupling_t[i] = dot_nt(wide_eye, coupling_parts[i])[:, :padded].astype(jnp.bfloat16)
    col_edge[...] = jnp.zeros_like(col_edge)
    col_own[...] = jnp.zeros_like(col_own)
    table[0:FRONT, :] = jnp.zeros((FRONT, LANES), jnp.float32)

    sides = (
        (row_edge, row_halo, 0, (lax.rem(gx + 1, nx), gy)),
        (row_edge, row_halo, 1, (lax.rem(gx + nx - 1, nx), gy)),
        (col_edge, col_halo, 0, (gx, lax.rem(gy + 1, ny))),
        (col_edge, col_halo, 1, (gx, lax.rem(gy + ny - 1, ny))),
    )
    inside = (gx > 0, gx < nx - 1, gy > 0, gy < ny - 1)
    ends = (pl.ds(0, levels, stride=rows_x), pl.ds(rows_x - 1, levels, stride=rows_x))

    def edge_copies(step):
        return [
            pltpu.make_async_remote_copy(
                src_ref=edge.at[step, which],
                dst_ref=halo.at[step, which],
                send_sem=edge_send.at[step, i],
                recv_sem=edge_recv.at[step, i],
                device_id=device,
                device_id_type=MESH,
            )
            for i, (edge, halo, which, device) in enumerate(sides)
        ]

    def row_values(step, which):
        return jnp.where(inside[which], row_halo[step, which, 0:levels, :], 0.0)

    vertical_mix(levels, rows_x, coupling_t, gradient, mixed)
    load_transport.wait()
    spread(levels, rows_x, transport, mixed, field, row_edge.at[0], col_edge.at[0], None, None)
    pl.semaphore_wait(barrier, ranks - 1)
    copies = edge_copies(0)
    for copy in copies:
        copy.start()
    vertical_mix(levels, rows_x, coupling_t, field, mixed)
    for copy in copies:
        copy.wait()
    both = jnp.concatenate([row_values(0, 0), row_values(0, 1)], axis=1)
    both = jnp.concatenate([both, jnp.zeros((padded - levels, 2 * LANES), jnp.float32)], axis=0)
    added = product((coupling_t[0], coupling_t[1]), split(both))
    for which in range(2):
        mixed[ends[which], :] = mixed[ends[which], :] + added[:levels, which * LANES : (which + 1) * LANES]
    strips = jnp.concatenate(
        [
            jnp.where(inside[2 + which], jnp.concatenate([col_halo[0, which, 0], col_halo[0, which, 1]], axis=1), 0.0)
            for which in range(2)
        ],
        axis=0,
    )
    strips = product(split(strips), coupling_parts)
    for which in range(2):
        for bank in range(2):
            col_mixed[which, bank] = strips[
                which * rows_x : (which + 1) * rows_x, bank * LANES : (bank + 1) * LANES
            ]

    spread(levels, rows_x, transport, mixed, field, row_edge.at[1], col_edge.at[1], col_mixed, col_own)
    copies = edge_copies(1)
    for copy in copies:
        copy.start()

    @pl.loop(0, (rows_x - 2) // 3)
    def _(t):
        for i in range(3):
            table_rows(levels, rows_x, field, table, 1 + t * 3 + i)

    slots_v[...] = slots_in[...] * 2
    load_slots = pltpu.make_async_copy(slots_v, slots, local_sem.at[2])
    load_slots.start()
    for copy in copies:
        copy.wait()
    corners = (
        (lax.broadcasted_iota(jnp.int32, (8, LANES), 0) * (LANES - 1) == lax.broadcasted_iota(jnp.int32, (8, LANES), 1))
        & (lax.broadcasted_iota(jnp.int32, (8, LANES), 0) < 2)
    ).astype(jnp.float32)
    for which in range(2):
        x = which * (rows_x - 1)
        halo = row_values(1, which)
        field[ends[which], :] = field[ends[which], :] + halo
        table_rows(levels, rows_x, field, table, x)
        halo = jnp.concatenate([halo, jnp.zeros((side - levels, LANES), jnp.float32)], axis=0)
        crossing = lax.dot_general(
            corners,
            halo,
            (((1,), (1,)), ((), ())),
            precision=lax.Precision.HIGHEST,
            preferred_element_type=jnp.float32,
        )
        for end in range(2):
            for bank in range(2):
                spot = col_own.at[end, bank]
                spot[x : x + 1, :] = spot[x : x + 1, :] + crossing[end : end + 1, bank * LANES : (bank + 1) * LANES]
    for end in range(2):
        for bank in range(2):
            strip = jnp.where(inside[2 + end], col_halo[1, end, bank], 0.0)
            col_mixed[end, bank] = strip
            table[pl.ds(FRONT + end * 2 * (LANES - 1) + bank, rows_x, stride=2 * LANES), :] = col_own[end, bank] + strip

    pick = identity(TAIL, jnp.bfloat16)

    def step_at(k):
        return lax.rem((k + 1) * STRIDE, ranks)

    def owner_at(k):
        tx, ty = peer(step_at(k))
        return tx * ny + ty

    def copy_for(k):
        step = step_at(k)
        tx, ty = peer(step)
        return pltpu.make_async_remote_copy(
            src_ref=outgoing.at[tx * ny + ty],
            dst_ref=received.at[me],
            send_sem=send_sem.at[step],
            recv_sem=recv_sem.at[step],
            device_id=(tx, ty),
            device_id_type=MESH,
        )

    def gather(k, rows):
        base = owner_at(k) * LANES
        for i in range(0, LANES, GROUP):
            got = [table[pl.ds(columns[base + i + j] * 2 + FRONT, 2), :] for j in range(GROUP)]
            for j in range(GROUP):
                rows[pl.ds((i + j) * 2, 2), :] = got[j]

    def pack(k, rows, next_k, next_rows):
        owner = owner_at(k)
        main = rows[pl.ds(0, LANES, stride=2), :].astype(jnp.bfloat16)
        tail = rows[pl.ds(1, LANES, stride=2), :].astype(jnp.bfloat16)
        packed = dot_nt(pick, tail)
        gather(next_k, next_rows)
        outgoing[owner, 0:MAIN, :] = main
        outgoing[owner, MAIN:BLOCK, :] = packed.astype(jnp.bfloat16)

    gather(0, ga)

    @pl.loop(0, ranks // 2)
    def _(t):
        k = t * 2
        pack(k, ga, k + 1, gb)
        copy_for(k).start()
        pack(k + 1, gb, jnp.minimum(k + 2, ranks - 1), ga)

        @pl.when(k + 1 < ranks - 1)
        def _():
            copy_for(k + 1).start()

    own = pltpu.make_async_copy(outgoing.at[me], received.at[me], local_sem.at[3])
    own.start()

    add_columns(levels, rows_x, field, col_mixed)
    part[...] = jnp.zeros_like(part)
    load_jac.wait()
    load_slots.wait()
    own.wait()

    spread_tail = identity(TAIL, jnp.bfloat16)

    def expand(h):
        base = pl.multiple_of(h * 2 * LANES, 2 * LANES)
        profiles[pl.ds(base, LANES, stride=2), :] = received[h, 0:MAIN, :].astype(jnp.float32)
        profiles[pl.ds(base + 1, LANES, stride=2), :] = lax.dot_general(
            received[h, MAIN:BLOCK, :], spread_tail, (((0,), (0,)), ((), ())), preferred_element_type=jnp.float32
        )

    def holder_at(k):
        hx, hy = moved(step_at(k), -1)
        return hx * ny + hy

    @pl.loop(0, ranks // EXPAND)
    def _(t):
        for i in range(EXPAND):
            k = t * EXPAND + i

            @pl.when(k < ranks - 1)
            def _():
                copy_for(k).wait_recv()

        for i in range(EXPAND):
            expand(holder_at(t * EXPAND + i))

    eye = identity(LANES, jnp.int32) == 1
    lane = lax.broadcasted_iota(jnp.int32, (1, LANES), 1)

    def fetch(j, rows, c, first, count):
        line = j * POINTS + c
        for i in range(first, first + count, GROUP):
            got = [profiles[pl.ds(slots[line, i + k], 2), :] for k in range(GROUP)]
            for k in range(GROUP):
                rows[pl.ds((c * LANES + i + k) * 2, 2), :] = got[k]

    def work(j, rows, next_j, next_rows):
        col = pl.multiple_of(j * LANES, LANES)
        tail = jnp.concatenate(
            [
                jac[MAIN:levels, pl.ds(col, LANES)].astype(jnp.float32),
                jnp.zeros((BLOCK - levels, LANES), jnp.float32),
            ],
            axis=0,
        ).astype(jnp.bfloat16)
        profile = jnp.concatenate(
            [jac[0:MAIN, pl.ds(col, LANES)], tail, jnp.zeros((2 * MAIN - BLOCK, LANES), jnp.bfloat16)], axis=0
        )
        value = jnp.zeros((1, LANES), jnp.float32)
        for c in range(POINTS):
            main = rows[pl.ds(c * 2 * LANES, LANES, stride=2), :].astype(jnp.bfloat16)
            rest = rows[pl.ds(c * 2 * LANES + 1, LANES, stride=2), :].astype(jnp.bfloat16)
            products = jnp.dot(
                jnp.concatenate([main, rest], axis=1), profile, preferred_element_type=jnp.float32
            )
            fetch(next_j, next_rows, c, 0, LANES // 2)
            diagonal = jnp.sum(jnp.where(eye, products, 0.0), axis=0, keepdims=True)
            value = value + diagonal * weight[c : c + 1, pl.ds(col, LANES)]
            fetch(next_j, next_rows, c, LANES // 2, LANES // 2)
        value = innovation[pl.ds(j, 1), :] * value
        value = jnp.where(lane + j * LANES < valid[0], value, 0.0)
        impact[pl.ds(j, 1), :] = value
        same = lax.broadcasted_iota(jnp.int32, (NI, LANES), 0) == inst[pl.ds(j, 1), :]
        part[...] += jnp.where(same, value, 0.0)

    for c in range(POINTS):
        fetch(0, oa, c, 0, LANES)

    @pl.loop(0, chunks // 2)
    def _(t):
        j = t * 2
        work(j, oa, j + 1, ob)
        work(j + 1, ob, jnp.minimum(j + 2, chunks - 1), oa)

    rows = lax.dot_general(
        jnp.ones((8, LANES), jnp.float32),
        part[...],
        (((1,), (1,)), ((), ())),
        precision=lax.Precision.HIGHEST,
        preferred_element_type=jnp.float32,
    )
    shares[me] = jnp.concatenate([rows, jnp.zeros((8, LANES - NI), jnp.float32)], axis=1)

    def share(k):
        return pltpu.make_async_remote_copy(
            src_ref=shares.at[me],
            dst_ref=shares.at[me],
            send_sem=share_send.at[k],
            recv_sem=share_recv.at[k],
            device_id=peer(k),
            device_id_type=MESH,
        )

    @pl.loop(1, ranks)
    def _(k):
        share(k).start()

    @pl.loop(0, ranks - 1)
    def _(k):
        copy_for(k).wait_send()

    @pl.loop(1, ranks)
    def _(k):
        share(k).wait()

    total[...] = jnp.sum(shares[...], axis=0)


def run(columns, valid, gradient, coupling, transport, jac, slots, weight, innovation, inst, ranks):
    levels, rows_x, lanes = gradient.shape
    count = innovation.shape[0]
    chunks = count // LANES
    flat = gradient.reshape(levels * rows_x, lanes)
    padded = -(-levels // TAIL) * TAIL
    slots = slots.reshape(POINTS, chunks, LANES).transpose(1, 0, 2).reshape(chunks * POINTS, LANES)
    f32, bf16 = jnp.float32, jnp.bfloat16
    row_edges = pltpu.VMEM((STEPS, 2, padded, LANES), f32)
    col_edges = pltpu.VMEM((STEPS, 2, 2, rows_x, LANES), f32)
    block = pltpu.VMEM((ranks, BLOCK, LANES), bf16)
    field, impact, total = pl.pallas_call(
        whole_kernel,
        out_shape=(
            jax.ShapeDtypeStruct(flat.shape, f32),
            jax.ShapeDtypeStruct((chunks, LANES), f32),
            jax.ShapeDtypeStruct((8, LANES), f32),
        ),
        in_specs=[SMEM, SMEM, VMEM, VMEM, ANY, ANY, VMEM, VMEM, VMEM, VMEM],
        out_specs=(VMEM, VMEM, VMEM),
        scratch_shapes=[
            pltpu.VMEM(transport.shape, bf16),
            pltpu.VMEM(jac.shape, bf16),
            pltpu.VMEM(slots.shape, jnp.int32),
            pltpu.SMEM(slots.shape, jnp.int32),
            pltpu.VMEM((2 * MAIN, 2 * MAIN), f32),
            pltpu.VMEM((2, padded, padded), bf16),
            pltpu.VMEM(flat.shape, f32),
            row_edges,
            col_edges,
            row_edges,
            col_edges,
            pltpu.VMEM((2, 2, rows_x, LANES), f32),
            pltpu.VMEM((2, 2, rows_x, LANES), f32),
            pltpu.VMEM((FRONT + rows_x * lanes * 2, LANES), f32),
            pltpu.VMEM((2 * LANES, LANES), f32),
            pltpu.VMEM((2 * LANES, LANES), f32),
            block,
            block,
            pltpu.VMEM((ranks * 2 * LANES, LANES), f32),
            pltpu.VMEM((POINTS * 2 * LANES, LANES), f32),
            pltpu.VMEM((POINTS * 2 * LANES, LANES), f32),
            pltpu.VMEM((NI, LANES), f32),
            pltpu.VMEM((ranks, 8, LANES), f32),
            pltpu.SemaphoreType.DMA((STEPS, 4)),
            pltpu.SemaphoreType.DMA((STEPS, 4)),
            pltpu.SemaphoreType.DMA((ranks,)),
            pltpu.SemaphoreType.DMA((ranks,)),
            pltpu.SemaphoreType.DMA((ranks,)),
            pltpu.SemaphoreType.DMA((ranks,)),
            pltpu.SemaphoreType.DMA((4,)),
        ],
        compiler_params=pltpu.CompilerParams(collective_id=1, has_side_effects=True, vmem_limit_bytes=58 * MIB),
        name="whole",
    )(
        columns,
        valid,
        flat,
        coupling,
        transport,
        jac,
        slots,
        weight,
        innovation.reshape(chunks, LANES),
        inst.reshape(chunks, LANES),
    )
    return field.reshape(gradient.shape), impact.reshape(count), total[0, :NI]


def body(
    gradient,
    coupling,
    transport,
    obs_jacobian,
    send_cols,
    obs_slots,
    obs_weight,
    obs_inst,
    innovation,
    valid_count,
):
    ranks = lax.axis_size("gx") * lax.axis_size("gy")
    return run(
        send_cols[0],
        valid_count,
        gradient,
        coupling,
        transport,
        obs_jacobian,
        obs_slots,
        obs_weight,
        innovation,
        obs_inst,
        ranks,
    )


def solution(mesh):
    placed = (
        P(None, "gx", "gy"),
        P(),
        P(None, None, "gx", "gy"),
        P(None, ("gx", "gy")),
        P(("gx", "gy"), None),
        P(None, ("gx", "gy")),
        P(None, ("gx", "gy")),
        P(("gx", "gy")),
        P(("gx", "gy")),
        P(("gx", "gy")),
    )
    return jax.shard_map(
        body,
        mesh=mesh,
        in_specs=placed,
        out_specs=(P(None, "gx", "gy"), P(("gx", "gy")), P()),
        check_vma=False,
    )
```

time: 166 us -> 151 us (0.910)
  Pallas kernels: 157 us -> 145 us
    pallas_call x3 -> x1, Pallas kernels: 157 us -> 145 us  [run(): pl.pallas_call(whole_kernel, out_shape=(jax.ShapeDtypeStruct(flat.shape,...]
    unnamed x16 -> x4, local copies, waits for them, and re-layouts: 4.63 us -> 3.82 us
where the time goes in v4:
time: 151 us
  Pallas kernels  145 us (96%)
  local copies, waits for them, and re-layouts  5.01 us (3%)
    pallas_call x1, Pallas kernels, run(): pl.pallas_call(whole_kernel, out_shape=(jax.ShapeDtypeStruct(flat.shape,...  145 us
    unnamed x4, local copies, waits for them, and re-layouts  3.82 us

profile of v4, /device:TPU:1, one launch (start us, length us, event | category | flops | bytes accessed | tf_op | source)
XLA Modules:
  0.0 150.9 jit_solution(7534226100049584555)
XLA Ops:
  1.3 144.6 %whole.1 = (f32[4384,128]{1,0:T(8,128)}, f32[64,128]{1,0:T(8,128)}, f32[8,128]{1,0:T(8,128)}) custom-call(s32[16384]{0:T(1024)} %bitcast.16, s32[1]{0:T(128)S(6)} %copy.16.valid, f32[4384,128]{1,0:T(8,128)} %bitcast.13, f32[137,137]{1,0:T(8,128)} %coupling.1, bf16[137,5,32,128]{3,2,1,0:T(8,128)(2,1)} %transport_in.1, bf16[137,8192]{1,0:T(8,128)(2,1)} %jac_in.1, ...), custom_call_target="tpu_custom_call" | custom-call | tf_op jit(solution)/shard_map/whole/pallas_call | solution.py:521
  145.9 1.2 slice_bitcast_fusion
  147.1 0.0 copy-start
  147.1 3.2 %copy.17 = f32[137,32,128]{2,1,0:T(8,128)} copy(f32[137,32,128]{2,1,0:T(8,128)} %bitcast.14) | data formatting | bytes 4489216
  150.3 0.0 copy-done
  150.3 0.6 copy.18
Async XLA Ops:
  147.1 3.2 %copy-start = (f32[64,128]{1,0:T(8,128)S(1)}, f32[64,128]{1,0:T(8,128)}, u32[]{:S(2)}) copy-start(f32[64,128]{1,0:T(8,128)} %get-tuple-element.7) | copy-start | bytes 98308

commit v5 on v4

--- a/solution.py
+++ b/solution.py
@@ -16,12 +16,14 @@
 MIX_UNROLL = 2
 FRONT = 8
 POINTS = 4
+PIECES = 4
+VLIM = 60
 EXPAND = 4
 STRIDE = 37
 MESH = pl.DeviceIdType.MESH
 VMEM = pl.BlockSpec(memory_space=pltpu.VMEM)
 SMEM = pl.BlockSpec(memory_space=pltpu.SMEM)
-ANY = pl.BlockSpec(memory_space=pl.ANY)
+HBM = pl.BlockSpec(memory_space=pltpu.HBM)
 MIB = 1024 * 1024
 
 
@@ -64,7 +66,7 @@
     return one + (two + jnp.dot(high_a, low_b, preferred_element_type=jnp.float32))
 
 
-def vertical_mix(levels, rows_x, coupling_t, source, mixed):
+def vertical_mix(levels, rows_x, coupling_t, source, mixed, beside=None):
     padded = coupling_t.shape[1]
     stacked = coupling_t[...].reshape(2 * padded, padded)
     pad = jnp.zeros((padded - levels, 2 * LANES), jnp.float32)
@@ -77,6 +79,8 @@
         )
         high, low = split(jnp.concatenate([pair, pad], axis=0))
         both = jnp.dot(stacked, high, preferred_element_type=jnp.float32)
+        if beside is not None:
+            beside(t)
         out = both[:padded] + (
             both[padded:] + jnp.dot(stacked[:padded], low, preferred_element_type=jnp.float32)
         )
@@ -169,21 +173,28 @@
 
 
 def whole_kernel(
-    columns,
+    columns_in,
     valid,
-    gradient,
-    coupling,
+    gradient_in,
+    coupling_in,
     transport_in,
     jac_in,
     slots_in,
+    weight_in,
+    innovation_in,
+    inst_in,
+    field_out,
+    impact,
+    total,
+    field,
+    columns,
+    gradient,
+    coupling,
+    transport,
+    jac,
     weight,
     innovation,
     inst,
-    field,
-    impact,
-    total,
-    transport,
-    jac,
     slots_v,
     slots,
     square,
@@ -204,7 +215,8 @@
     oa,
     ob,
     part,
-    shares,
+    near_shares,
+    far_shares,
     edge_send,
     edge_recv,
     send_sem,
@@ -223,16 +235,39 @@
     chunks = impact.shape[0]
     barrier = pltpu.get_barrier_semaphore()
 
-    load_transport = pltpu.make_async_copy(transport_in, transport, local_sem.at[0])
-    load_transport.start()
-    load_jac = pltpu.make_async_copy(jac_in, jac, local_sem.at[1])
-    load_jac.start()
-
-    @pl.loop(1, ranks)
-    def _(k):
+    loads = [
+        pltpu.make_async_copy(source, target, local_sem.at[4 + i])
+        for i, (source, target) in enumerate(
+            (
+                (coupling_in, coupling),
+                (gradient_in, gradient),
+                (transport_in, transport),
+                (slots_in, slots_v),
+                (columns_in, columns),
+                (jac_in, jac),
+                (weight_in, weight),
+                (innovation_in, innovation),
+                (inst_in, inst),
+            )
+        )
+    ]
+    for load in loads:
+        load.start()
+    load_coupling, load_gradient, load_transport, load_lines, load_columns = loads[:5]
+
+    def greet(k):
         pl.semaphore_signal(barrier, inc=1, device_id=peer(k), device_id_type=MESH)
 
+    share_of = ranks // (rows_x // 2)
+    for k in range(share_of, ranks, share_of):
+        greet(k)
+
+    def greet_some(t):
+        for i in range(1, share_of):
+            greet(t * share_of + i)
+
     square[...] = jnp.zeros_like(square)
+    load_coupling.wait()
     square[0:levels, 0:levels] = coupling[...]
     coupling_parts = split(square[...])
     side = square.shape[0]
@@ -270,7 +305,8 @@
     def row_values(step, which):
         return jnp.where(inside[which], row_halo[step, which, 0:levels, :], 0.0)
 
-    vertical_mix(levels, rows_x, coupling_t, gradient, mixed)
+    load_gradient.wait()
+    vertical_mix(levels, rows_x, coupling_t, gradient, mixed, greet_some)
     load_transport.wait()
     spread(levels, rows_x, transport, mixed, field, row_edge.at[0], col_edge.at[0], None, None)
     pl.semaphore_wait(barrier, ranks - 1)
@@ -309,7 +345,9 @@
         for i in range(3):
             table_rows(levels, rows_x, field, table, 1 + t * 3 + i)
 
-    slots_v[...] = slots_in[...] * 2
+    load_lines.wait()
+    slots_v[...] = slots_v[...] * 2
+    load_columns.wait()
     load_slots = pltpu.make_async_copy(slots_v, slots, local_sem.at[2])
     load_slots.start()
     for copy in copies:
@@ -356,7 +394,7 @@
         return pltpu.make_async_remote_copy(
             src_ref=outgoing.at[tx * ny + ty],
             dst_ref=received.at[me],
-            send_sem=send_sem.at[step],
+            send_sem=send_sem,
             recv_sem=recv_sem.at[step],
             device_id=(tx, ty),
             device_id_type=MESH,
@@ -395,8 +433,11 @@
     own.start()
 
     add_columns(levels, rows_x, field, col_mixed)
+    store_field = pltpu.make_async_copy(field, field_out, local_sem.at[0])
+    store_field.start()
     part[...] = jnp.zeros_like(part)
-    load_jac.wait()
+    for load in loads[5:]:
+        load.wait()
     load_slots.wait()
     own.wait()
 
@@ -473,6 +514,15 @@
         work(j, oa, j + 1, ob)
         work(j + 1, ob, jnp.minimum(j + 2, chunks - 1), oa)
 
+    pltpu.make_async_remote_copy(
+        src_ref=outgoing.at[pl.ds(0, ranks - 1)],
+        dst_ref=received.at[pl.ds(0, ranks - 1)],
+        send_sem=send_sem,
+        recv_sem=recv_sem.at[0],
+        device_id=peer(1),
+        device_id_type=MESH,
+    ).wait_send()
+
     rows = lax.dot_general(
         jnp.ones((8, LANES), jnp.float32),
         part[...],
@@ -480,34 +530,34 @@
         precision=lax.Precision.HIGHEST,
         preferred_element_type=jnp.float32,
     )
-    shares[me] = jnp.concatenate([rows, jnp.zeros((8, LANES - NI), jnp.float32)], axis=1)
-
-    def share(k):
-        return pltpu.make_async_remote_copy(
-            src_ref=shares.at[me],
-            dst_ref=shares.at[me],
-            send_sem=share_send.at[k],
-            recv_sem=share_recv.at[k],
-            device_id=peer(k),
-            device_id_type=MESH,
-        )
-
-    @pl.loop(1, ranks)
-    def _(k):
-        share(k).start()
-
-    @pl.loop(0, ranks - 1)
-    def _(k):
-        copy_for(k).wait_send()
-
-    @pl.loop(1, ranks)
-    def _(k):
-        share(k).wait()
-
-    total[...] = jnp.sum(shares[...], axis=0)
-
-
-def run(columns, valid, gradient, coupling, transport, jac, slots, weight, innovation, inst, ranks):
+    own_rows = jnp.concatenate([rows, jnp.zeros((8, LANES - NI), jnp.float32)], axis=1)
+
+    def share(value, slots_at, size, mine, device, base):
+        slots_at[mine] = value
+        shared = [
+            pltpu.make_async_remote_copy(
+                src_ref=slots_at.at[mine],
+                dst_ref=slots_at.at[mine],
+                send_sem=share_send.at[base + k],
+                recv_sem=share_recv.at[base + k],
+                device_id=device(lax.rem(mine + k, size)),
+                device_id_type=MESH,
+            )
+            for k in range(1, size)
+        ]
+        for copy in shared:
+            copy.start()
+        for copy in shared:
+            copy.wait()
+        return jnp.sum(slots_at[...], axis=0)
+
+    store_field.wait()
+    near = share(own_rows, near_shares, ny, gy, lambda i: (gx, i), 0)
+    total[...] = share(near, far_shares, nx, gx, lambda i: (i, gy), ny)[0:1, :NI]
+
+
+def run(columns, valid, gradient, coupling, transport, jac, slots, weight, innovation, inst, nx, ny):
+    ranks = nx * ny
     levels, rows_x, lanes = gradient.shape
     count = innovation.shape[0]
     chunks = count // LANES
@@ -523,13 +573,20 @@
         out_shape=(
             jax.ShapeDtypeStruct(flat.shape, f32),
             jax.ShapeDtypeStruct((chunks, LANES), f32),
-            jax.ShapeDtypeStruct((8, LANES), f32),
+            jax.ShapeDtypeStruct((1, NI), f32),
         ),
-        in_specs=[SMEM, SMEM, VMEM, VMEM, ANY, ANY, VMEM, VMEM, VMEM, VMEM],
-        out_specs=(VMEM, VMEM, VMEM),
+        in_specs=[HBM, SMEM] + [HBM] * 8,
+        out_specs=(HBM, VMEM, VMEM),
         scratch_shapes=[
+            pltpu.VMEM(flat.shape, f32),
+            pltpu.SMEM(columns.shape, jnp.int32),
+            pltpu.VMEM(flat.shape, f32),
+            pltpu.VMEM(coupling.shape, f32),
             pltpu.VMEM(transport.shape, bf16),
             pltpu.VMEM(jac.shape, bf16),
+            pltpu.VMEM(weight.shape, f32),
+            pltpu.VMEM((chunks, LANES), f32),
+            pltpu.VMEM((chunks, LANES), jnp.int32),
             pltpu.VMEM(slots.shape, jnp.int32),
             pltpu.SMEM(slots.shape, jnp.int32),
             pltpu.VMEM((2 * MAIN, 2 * MAIN), f32),
@@ -550,16 +607,17 @@
             pltpu.VMEM((POINTS * 2 * LANES, LANES), f32),
             pltpu.VMEM((POINTS * 2 * LANES, LANES), f32),
             pltpu.VMEM((NI, LANES), f32),
-            pltpu.VMEM((ranks, 8, LANES), f32),
+            pltpu.VMEM((ny, 8, LANES), f32),
+            pltpu.VMEM((nx, 8, LANES), f32),
             pltpu.SemaphoreType.DMA((STEPS, 4)),
             pltpu.SemaphoreType.DMA((STEPS, 4)),
+            pltpu.SemaphoreType.DMA,
             pltpu.SemaphoreType.DMA((ranks,)),
-            pltpu.SemaphoreType.DMA((ranks,)),
-            pltpu.SemaphoreType.DMA((ranks,)),
-            pltpu.SemaphoreType.DMA((ranks,)),
-            pltpu.SemaphoreType.DMA((4,)),
+            pltpu.SemaphoreType.DMA((nx + ny,)),
+            pltpu.SemaphoreType.DMA((nx + ny,)),
+            pltpu.SemaphoreType.DMA((13,)),
         ],
-        compiler_params=pltpu.CompilerParams(collective_id=1, has_side_effects=True, vmem_limit_bytes=58 * MIB),
+        compiler_params=pltpu.CompilerParams(collective_id=1, has_side_effects=True, vmem_limit_bytes=VLIM * MIB),
         name="whole",
     )(
         columns,
@@ -573,7 +631,40 @@
         innovation.reshape(chunks, LANES),
         inst.reshape(chunks, LANES),
     )
-    return field.reshape(gradient.shape), impact.reshape(count), total[0, :NI]
+    field, impact, total = finish(field, impact, total)
+    return field.reshape(gradient.shape), impact.reshape(count), total.reshape(NI)
+
+
+def finish_kernel(field, impact, total, field_out, impact_out, total_out, held, in_sem, out_sem):
+    size = field.shape[0] // PIECES
+    cuts = [pl.ds(i * size, size) for i in range(PIECES)]
+    ins = [pltpu.make_async_copy(field.at[cut], held.at[cut], in_sem.at[i]) for i, cut in enumerate(cuts)]
+    outs = [pltpu.make_async_copy(held.at[cut], field_out.at[cut], out_sem.at[i]) for i, cut in enumerate(cuts)]
+    for copy in ins:
+        copy.start()
+    impact_out[...] = impact[...]
+    total_out[...] = total[...]
+    for come, go in zip(ins, outs):
+        come.wait()
+        go.start()
+    for copy in outs:
+        copy.wait()
+
+
+def finish(field, impact, total):
+    return pl.pallas_call(
+        finish_kernel,
+        out_shape=tuple(jax.ShapeDtypeStruct(a.shape, a.dtype) for a in (field, impact, total)),
+        in_specs=[HBM, VMEM, VMEM],
+        out_specs=(HBM, VMEM, VMEM),
+        scratch_shapes=[
+            pltpu.VMEM(field.shape, field.dtype),
+            pltpu.SemaphoreType.DMA((PIECES,)),
+            pltpu.SemaphoreType.DMA((PIECES,)),
+        ],
+        compiler_params=pltpu.CompilerParams(vmem_limit_bytes=VLIM * MIB),
+        name="finish",
+    )(field, impact, total)
 
 
 def body(
@@ -588,7 +679,6 @@
     innovation,
     valid_count,
 ):
-    ranks = lax.axis_size("gx") * lax.axis_size("gy")
     return run(
         send_cols[0],
         valid_count,
@@ -600,7 +690,8 @@
         obs_weight,
         innovation,
         obs_inst,
-        ranks,
+        lax.axis_size("gx"),
+        lax.axis_size("gy"),
     )
 
 

time: 151 us -> 142 us (0.940)
  local copies, waits for them, and re-layouts: 5.01 us -> 0 us
  Pallas kernels: 145 us -> 141 us
    pallas_call x1, Pallas kernels: 145 us -> 137 us  [run(): pl.pallas_call(whole_kernel, out_shape=(jax.ShapeDtypeStruct(flat.shape,...]
    pallas_call x0 -> x1, Pallas kernels: none -> 3.86 us  [finish(): pl.pallas_call(finish_kernel, out_shape=tuple((jax.ShapeDtypeStruct(a.sha...]
    unnamed x4 -> x0, local copies, waits for them, and re-layouts: 3.82 us -> none
where the time goes in v5:
time: 142 us
  Pallas kernels  141 us (99%)
    pallas_call x1, Pallas kernels, run(): pl.pallas_call(whole_kernel, out_shape=(jax.ShapeDtypeStruct(flat.shape,...  137 us
    pallas_call x1, Pallas kernels, finish(): pl.pallas_call(finish_kernel, out_shape=tuple((jax.ShapeDtypeStruct(a.sha...  3.86 us

profile of v5, /device:TPU:1, one launch (start us, length us, event | category | flops | bytes accessed | tf_op | source)
XLA Modules:
  0.0 142.3 jit_solution(5328682101021426641)
XLA Ops:
  1.3 137.1 %whole.1 = (f32[4384,128]{1,0:T(8,128)}, f32[64,128]{1,0:T(8,128)}, f32[1,32]{1,0:T(1,128)}) custom-call(s32[16384]{0:T(1024)} %bitcast.14, s32[1]{0:T(128)S(6)} %copy.14.valid, f32[4384,128]{1,0:T(8,128)} %bitcast.12, f32[137,137]{1,0:T(8,128)} %coupling_in.1, bf16[137,5,32,128]{3,2,1,0:T(8,128)(2,1)} %transport_in.1, bf16[137,8192]{1,0:T(8,128)(2,1)} %jac_in.1, ...), custom_call_target="tpu_custom_call" | custom-call | tf_op jit(solution)/shard_map/whole/pallas_call | solution.py:571
  138.4 3.9 %finish.1 = (f32[4384,128]{1,0:T(8,128)}, f32[64,128]{1,0:T(8,128)}, f32[1,32]{1,0:T(1,128)}) custom-call(f32[4384,128]{1,0:T(8,128)} %get-tuple-element.9.field, f32[64,128]{1,0:T(8,128)} %get-tuple-element.10.impact, f32[1,32]{1,0:T(1,128)} %get-tuple-element.11.total), custom_call_target="tpu_custom_call" | custom-call | tf_op jit(solution)/shard_map/finish/pallas_call | solution.py:655

commit v6 on v5

--- a/solution.py
+++ b/solution.py
@@ -13,7 +13,7 @@
 BLOCK = MAIN + TAIL
 GROUP = 8
 WIDE = 8
-MIX_UNROLL = 2
+MIX_UNROLL = 4
 FRONT = 8
 POINTS = 4
 PIECES = 4
@@ -88,17 +88,17 @@
         mixed[pl.ds(x + 1, levels, stride=rows_x), :] = out[:levels, LANES:]
 
 
-def by_bank(levels, work):
+def by_bank(levels, work, wide):
     for bank, first in enumerate(range(0, levels, LANES)):
         count = min(LANES, levels - first)
-        whole = count // WIDE
+        whole = count // wide
 
         @pl.loop(0, whole)
         def _(t):
-            work(bank, first, t * WIDE, WIDE)
-
-        if count % WIDE:
-            work(bank, first, whole * WIDE, count % WIDE)
+            work(bank, first, t * wide, wide)
+
+        if count % wide:
+            work(bank, first, whole * wide, count % wide)
 
 
 def at_edges(lane, first, last):
@@ -145,7 +145,7 @@
             col_own[0, bank] = first_own
             col_own[1, bank] = last_own
 
-    by_bank(levels, work)
+    by_bank(levels, work, WIDE if col_mixed is None else WIDE // 2)
 
 
 def add_columns(levels, rows_x, out, col_halo):
@@ -160,7 +160,7 @@
             after = pltpu.roll(after_all, LANES - 1 - at, 1)
             out[here, :] = out[here, :] + at_edges(lane, before, after)
 
-    by_bank(levels, work)
+    by_bank(levels, work, WIDE)
 
 
 def table_rows(levels, rows_x, field, table, x):
@@ -470,9 +470,9 @@
     lane = lax.broadcasted_iota(jnp.int32, (1, LANES), 1)
 
     def fetch(j, rows, c, first, count):
-        line = j * POINTS + c
+        line = j * (POINTS * LANES) + c * LANES
         for i in range(first, first + count, GROUP):
-            got = [profiles[pl.ds(slots[line, i + k], 2), :] for k in range(GROUP)]
+            got = [profiles[pl.ds(slots[line + i + k], 2), :] for k in range(GROUP)]
             for k in range(GROUP):
                 rows[pl.ds((c * LANES + i + k) * 2, 2), :] = got[k]
 
@@ -563,7 +563,7 @@
     chunks = count // LANES
     flat = gradient.reshape(levels * rows_x, lanes)
     padded = -(-levels // TAIL) * TAIL
-    slots = slots.reshape(POINTS, chunks, LANES).transpose(1, 0, 2).reshape(chunks * POINTS, LANES)
+    slots = slots.reshape(POINTS, chunks, LANES).transpose(1, 0, 2).reshape(chunks * POINTS * LANES)
     f32, bf16 = jnp.float32, jnp.bfloat16
     row_edges = pltpu.VMEM((STEPS, 2, padded, LANES), f32)
     col_edges = pltpu.VMEM((STEPS, 2, 2, rows_x, LANES), f32)

time: 142 us -> 141 us (level)
  Pallas kernels: 141 us -> 139 us
    pallas_call x1, Pallas kernels: 137 us -> 136 us  [run(): pl.pallas_call(whole_kernel, out_shape=(jax.ShapeDtypeStruct(flat.shape,...]
where the time goes in v6:
time: 141 us
  Pallas kernels  139 us (99%)
    pallas_call x1, Pallas kernels, run(): pl.pallas_call(whole_kernel, out_shape=(jax.ShapeDtypeStruct(flat.shape,...  136 us
    pallas_call x1, Pallas kernels, finish(): pl.pallas_call(finish_kernel, out_shape=tuple((jax.ShapeDtypeStruct(a.sha...  3.86 us

profile of v6, /device:TPU:1, one launch (start us, length us, event | category | flops | bytes accessed | tf_op | source)
XLA Modules:
  0.0 140.7 jit_solution(5224210413243824198)
XLA Ops:
  1.3 135.6 %whole.1 = (f32[4384,128]{1,0:T(8,128)}, f32[64,128]{1,0:T(8,128)}, f32[1,32]{1,0:T(1,128)}) custom-call(s32[16384]{0:T(1024)} %bitcast.14, s32[1]{0:T(128)S(6)} %copy.14.valid, f32[4384,128]{1,0:T(8,128)} %bitcast.12, f32[137,137]{1,0:T(8,128)} %coupling_in.1, bf16[137,5,32,128]{3,2,1,0:T(8,128)(2,1)} %transport_in.1, bf16[137,8192]{1,0:T(8,128)(2,1)} %jac_in.1, ...), custom_call_target="tpu_custom_call" | custom-call | tf_op jit(solution)/shard_map/whole/pallas_call | solution.py:571
  136.9 3.9 %finish.1 = (f32[4384,128]{1,0:T(8,128)}, f32[64,128]{1,0:T(8,128)}, f32[1,32]{1,0:T(1,128)}) custom-call(f32[4384,128]{1,0:T(8,128)} %get-tuple-element.9.field, f32[64,128]{1,0:T(8,128)} %get-tuple-element.10.impact, f32[1,32]{1,0:T(1,128)} %get-tuple-element.11.total), custom_call_target="tpu_custom_call" | custom-call | tf_op jit(solution)/shard_map/finish/pallas_call | solution.py:655
